TPU v7x, 512 devices: a whole 4x4x16 slice. The times are simulated.
512 devices in a mesh: lon: 32 (over x, z_lo), lat: 16 (over z_hi, y, core).
Axes of the slice: x: 4, y: 4, z: 16 (z_hi: 2, z_lo: 8; z = z_hi * 8 + z_lo), core: 2. Of those that a mesh axis runs over, the one named last changes fastest.
Arguments:
- ensemble_state: bfloat16 [512, 2048, 256], P('lat', 'lon'), may hold values from -6 to 6
- courant: float32 [2, 512, 2048], P(None, 'lat', 'lon'), may hold values from -0.45 to 0.45
- obs_where: int32 [2, 3, 128], replicated, may hold values from 0 to 2047, as said below
- obs_value: float32 [2, 128], replicated, may hold values from -6 to 6
- obs_variance: float32 [2, 128], replicated, may hold values from 0.25 to 2
- obs_noise: float32 [2, 128, 256], replicated, may hold values from -5 to 5
Outputs:
- analysis: bfloat16 [512, 2048, 256], P('lat', 'lon')
Inputs may be any that keep to these rules, and one draw needn't show every extreme that they name: `obs_where`: row 0 holds latitude rows, row 1 longitude columns, row 2 radii of 24 to 96 cells; observations cluster around a few centres per batch, the rest spread over the grid.
All inputs are finite; a program needn't handle non-finite values.
Results may differ from a plain program's by a relative error of at most 0.001.
Values sent between devices are 32-bit elements; how exact they have to be, the bound alone decides.
A program may use at most 64 MiB of HBM per device.

v0:
```python
import jax
import jax.numpy as jnp
from jax import lax
from jax.sharding import PartitionSpec as P

BATCHES = 2
ADV_STEPS = 2


def extended(block, sides, width):
    for axis, dim in sides:
        count = lax.axis_size(axis)
        forward = [(i, i + 1) for i in range(count - 1)]
        forward.append((count - 1, 0))
        backward = [(target, source) for source, target in forward]
        low = lax.ppermute(
            lax.slice_in_dim(block, block.shape[dim] - width, None, axis=dim), axis, forward
        )
        high = lax.ppermute(lax.slice_in_dim(block, 0, width, axis=dim), axis, backward)
        block = jnp.concatenate([low, block, high], axis=dim)
    return block


def matmul_exact(left, right):
    return jnp.dot(left, right, precision=lax.Precision.HIGHEST, preferred_element_type=jnp.float32)


def combine_upwind(grid_field, below_rows, above_rows, west_side, east_side, speed_lat, speed_lon):
    lat_plus = jnp.maximum(speed_lat, 0.0)[..., None]
    lat_minus = jnp.minimum(speed_lat, 0.0)[..., None]
    lon_plus = jnp.maximum(speed_lon, 0.0)[..., None]
    lon_minus = jnp.minimum(speed_lon, 0.0)[..., None]
    return (
        grid_field
        - lat_plus * (grid_field - below_rows)
        - lat_minus * (above_rows - grid_field)
        - lon_plus * (grid_field - west_side)
        - lon_minus * (east_side - grid_field)
    )


def advance(padded, speed_lat, speed_lon):
    return combine_upwind(
        padded[1:-1, 1:-1],
        padded[:-2, 1:-1],
        padded[2:, 1:-1],
        padded[1:-1, :-2],
        padded[1:-1, 2:],
        speed_lat,
        speed_lon,
    )


def clear_outside(padded, row_start, total_rows, margin):
    global_rows = row_start - margin + jnp.arange(padded.shape[0], dtype=jnp.int32)
    inside = ((global_rows >= 0) & (global_rows < total_rows)).astype(padded.dtype)
    return padded * inside[:, None, None]


def taper_weights(cell_lat, cell_lon, obs_lat, obs_lon, radius, width):
    lat_gap = cell_lat - obs_lat
    lon_gap = jnp.abs(cell_lon - obs_lon)
    lon_gap = jnp.minimum(lon_gap, width - lon_gap)
    distance_sq = (lat_gap * lat_gap + lon_gap * lon_gap).astype(jnp.float32)
    radius_sq = (radius * radius).astype(jnp.float32)
    return jnp.square(jnp.maximum(1.0 - distance_sq / radius_sq, 0.0))


def batch_weights(priors, values, variance, noise):
    members = priors.shape[1]
    anomaly = priors - jnp.mean(priors, axis=1, keepdims=True)
    system = matmul_exact(anomaly, anomaly.T) / (members - 1) + jnp.diag(variance)
    misfit = values[:, None] + jnp.sqrt(variance)[:, None] * noise - priors
    factor = jnp.linalg.cholesky(system)
    halfway = lax.linalg.triangular_solve(factor, misfit, left_side=True, lower=True)
    weights = lax.linalg.triangular_solve(
        factor, halfway, left_side=True, lower=True, transpose_a=True
    )
    return (anomaly, weights)


def body(ensemble_state, courant, obs_where, obs_value, obs_variance, obs_noise):
    rows_tile, cols_tile, members = ensemble_state.shape
    total_rows = rows_tile * lax.axis_size("lat")
    total_cols = cols_tile * lax.axis_size("lon")
    row_start = lax.axis_index("lat") * rows_tile
    col_start = lax.axis_index("lon") * cols_tile
    grid_field = ensemble_state.astype(jnp.float32)
    for step_index in range(ADV_STEPS):
        padded = extended(grid_field, (("lon", 1), ("lat", 0)), 1)
        padded = clear_outside(padded, row_start, total_rows, 1)
        grid_field = advance(padded, courant[0], courant[1])
    ensemble = grid_field.reshape(rows_tile * cols_tile, members)
    cell_index = jnp.arange(rows_tile * cols_tile, dtype=jnp.int32)
    cell_lat = (row_start + cell_index // cols_tile)[:, None]
    cell_lon = (col_start + cell_index % cols_tile)[:, None]
    for batch_index in range(BATCHES):
        obs_lat = obs_where[batch_index, 0]
        obs_lon = obs_where[batch_index, 1]
        local_index = (obs_lat - row_start) * cols_tile + (obs_lon - col_start)
        owned_mask = (
            (obs_lat >= row_start)
            & (obs_lat < row_start + rows_tile)
            & (obs_lon >= col_start)
            & (obs_lon < col_start + cols_tile)
        )
        priors = lax.psum(
            matmul_exact(
                ((local_index[:, None] == cell_index[None, :]) & owned_mask[:, None]).astype(
                    jnp.float32
                ),
                ensemble,
            ),
            ("lon", "lat"),
        )
        anomaly_obs, weights = batch_weights(
            priors, obs_value[batch_index], obs_variance[batch_index], obs_noise[batch_index]
        )
        weight_map = taper_weights(
            cell_lat,
            cell_lon,
            obs_where[batch_index, 0][None, :],
            obs_where[batch_index, 1][None, :],
            obs_where[batch_index, 2][None, :],
            total_cols,
        )
        anomaly = ensemble - jnp.mean(ensemble, axis=1, keepdims=True)
        covariance = matmul_exact(anomaly, anomaly_obs.T) / (members - 1)
        ensemble = ensemble + matmul_exact(weight_map * covariance, weights)
    return ensemble.reshape(rows_tile, cols_tile, members).astype(jnp.bfloat16)


def solution(mesh):
    placed = (P("lat", "lon", None), P(None, "lat", "lon"), P(), P(), P(), P())
    return jax.shard_map(
        body, mesh=mesh, in_specs=placed, out_specs=P("lat", "lon", None), check_vma=False
    )
```

profile of v0, /device:TPU:1, one launch (start us, length us, event | category | flops | bytes accessed | tf_op | source)
XLA Modules:
  0.0 1062.7 jit_solution(13761591134135253996)
XLA Ops:
  6.5 1.0 fusion.95
  7.6 4.4 collective-permute-start
  11.9 13.4 %collective-permute-start.1 = (f32[32,1,256]{2,1,0:T(1,128)S(1)}, f32[32,1,256]{2,1,0:T(1,128)S(1)}, u32[]{:S(2)}, u32[]{:S(2)}) collective-permute-start(f32[32,1,256]{2,1,0:T(1,128)S(1)} %get-tuple-element.17), channel_id=1, source_target_pairs={{16,0},{32,16},{48,32},{64,48},{80,64},{96,80},{112,96},{128,112},... | collective-permute-start | bytes 98312 | tf_op jit(solution)/shard_map/ppermute | solution.py:19
  25.4 0.8 slice_bitcast_fusion.1
  26.2 0.8 fusion.91
  26.9 0.8 slice_bitcast_fusion
  27.7 0.8 slice_bitcast_fusion.3
  28.4 0.7 maximum_bitcast_fusion.1
  29.2 0.8 subtract_add_fusion
  30.0 1.5 convert_element_type.47
  31.5 4.0 collective-permute-start.2
  35.5 3.4 collective-permute-start.3
  39.0 2.2 collective-permute-done.3
  41.2 0.3 maximum_multiply_fusion
  41.5 2.1 fusion.12
  43.6 1.9 collective-permute-start.4
  45.6 12.1 %collective-permute-start.5 = (f32[32,1,256]{2,1,0:T(1,128)S(1)}, f32[32,1,256]{2,1,0:T(1,128)S(1)}, u32[]{:S(2)}, u32[]{:S(2)}) collective-permute-start(f32[32,1,256]{2,1,0:T(1,128)S(1)} %get-tuple-element.15), channel_id=1, source_target_pairs={{16,0},{32,16},{48,32},{64,48},{80,64},{96,80},{112,96},{128,112},... | collective-permute-start | bytes 98312 | tf_op jit(solution)/shard_map/ppermute | solution.py:19
  57.7 0.3 collective-permute-done.4
  58.0 0.7 collective-permute-done.5
  58.7 3.0 collective-permute-start.6
  61.7 14.7 %collective-permute-start.7 = (f32[1,66,256]{2,1,0:T(8,128)S(1)}, f32[1,66,256]{2,1,0:T(8,128)S(1)}, u32[]{:S(2)}, u32[]{:S(2)}) collective-permute-start(f32[1,66,256]{2,1,0:T(8,128)S(1)} %get-tuple-element.11), channel_id=1, source_target_pairs={{1,0},{2,1},{3,2},{4,3},{5,4},{6,5},{7,6},{8,7},{9,8},{10,9},{11,1... | collective-permute-start | bytes 202760 | tf_op jit(solution)/shard_map/ppermute | solution.py:19
  76.4 0.9 collective-permute-done.7
  77.3 0.3 maximum_multiply_fusion.1
  77.6 2.5 fusion.92
  80.2 1.7 fusion.40
  82.2 467.7 %all-reduce.3.cloned.1.call-done = f32[128,256]{1,0:T(8,128)} async-done(((f32[128,256]{1,0:T(8,128)}), f32[128,256]{1,0:T(8,128)}) %all-reduce.3.cloned.1.call-update) | async-done | bytes 131088 | tf_op jit(solution)/shard_map/psum | solution.py:107
  549.8 1.0 reduce_sum.37
  550.8 1.3 fusion.21
  552.3 11.7 %cholesky.44 = f32[128,128]{1,0:T(8,128)S(1)} custom-call(f32[128,128]{1,0:T(8,128)S(1)} %fusion.72), custom_call_target="Cholesky" | custom-call | tf_op jit(solution)/shard_map/jit(cholesky)/cholesky | solution.py:74
  564.0 0.6 compare_reduce_fusion.1
  564.7 0.7 fusion.63
  565.3 9.8 custom-call.11
  575.2 1.3 fusion.55
  576.4 0.3 fusion.70
  576.7 3.0 fusion.2
  579.7 3.5 fusion.96
  583.1 1.7 fusion.43
  584.8 438.2 %all-reduce.5.cloned.1.call-done = f32[128,256]{1,0:T(8,128)} async-done(((f32[128,256]{1,0:T(8,128)}), f32[128,256]{1,0:T(8,128)}) %all-reduce.5.cloned.1.call-update) | async-done | bytes 131088 | tf_op jit(solution)/shard_map/psum | solution.py:107
  1023.1 1.0 reduce_sum.39
  1024.1 1.5 fusion.22
  1025.8 11.7 %cholesky.55 = f32[128,128]{1,0:T(8,128)S(1)} custom-call(f32[128,128]{1,0:T(8,128)S(1)} %fusion.68), custom_call_target="Cholesky" | custom-call | tf_op jit(solution)/shard_map/jit(cholesky)/cholesky | solution.py:74
  1037.5 0.6 compare_reduce_fusion
  1038.2 0.7 fusion.64
  1038.8 9.8 custom-call.13
  1048.6 1.3 fusion.51
  1049.9 0.3 fusion.66
  1050.2 3.0 fusion.1
  1053.1 2.8 fusion
  (31 shorter events, 0.8 us)
Async XLA Ops:
  6.5 543.3 %all-reduce.3.cloned.1.call-start = ((), (), s32[]{:S(2)}) async-start(), calls=%async_computation | async-start | bytes 262144 | tf_op jit(solution)/shard_map/psum | solution.py:107
  7.6 23.9 %collective-permute-start = (f32[32,1,256]{2,1,0:T(1,128)S(1)}, f32[32,1,256]{2,1,0:T(1,128)S(1)}, u32[]{:S(2)}, u32[]{:S(2)}) collective-permute-start(f32[32,1,256]{2,1,0:T(1,128)S(1)} %get-tuple-element.16), channel_id=1, source_target_pairs={{0,16},{16,32},{32,48},{48,64},{64,80},{80,96},{96,112},{112,128},... | collective-permute-start | bytes 98312 | tf_op jit(solution)/shard_map/ppermute | solution.py:16
  11.9 19.5 %collective-permute-start.1 = (f32[32,1,256]{2,1,0:T(1,128)S(1)}, f32[32,1,256]{2,1,0:T(1,128)S(1)}, u32[]{:S(2)}, u32[]{:S(2)}) collective-permute-start(f32[32,1,256]{2,1,0:T(1,128)S(1)} %get-tuple-element.17), channel_id=1, source_target_pairs={{16,0},{32,16},{48,32},{64,48},{80,64},{96,80},{112,96},{128,112},... | collective-permute-start | bytes 98312 | tf_op jit(solution)/shard_map/ppermute | solution.py:19
  31.5 7.5 collective-permute-start.2
  35.5 5.7 collective-permute-start.3
  41.5 16.1 %copy-start.2 = (s32[2,3,128]{2,0,1:T(2,128)S(1)}, s32[2,3,128]{2,0,1:T(2,128)}, u32[]{:S(2)}) copy-start(s32[2,3,128]{2,0,1:T(2,128)} %param.13) | copy-start | bytes 9220
  43.6 14.3 %collective-permute-start.4 = (f32[32,1,256]{2,1,0:T(1,128)S(1)}, f32[32,1,256]{2,1,0:T(1,128)S(1)}, u32[]{:S(2)}, u32[]{:S(2)}) collective-permute-start(f32[32,1,256]{2,1,0:T(1,128)S(1)} %get-tuple-element.14), channel_id=1, source_target_pairs={{0,16},{16,32},{32,48},{48,64},{64,80},{80,96},{96,112},{112,128},... | collective-permute-start | bytes 98312 | tf_op jit(solution)/shard_map/ppermute | solution.py:16
  45.6 13.1 %collective-permute-start.5 = (f32[32,1,256]{2,1,0:T(1,128)S(1)}, f32[32,1,256]{2,1,0:T(1,128)S(1)}, u32[]{:S(2)}, u32[]{:S(2)}) collective-permute-start(f32[32,1,256]{2,1,0:T(1,128)S(1)} %get-tuple-element.15), channel_id=1, source_target_pairs={{16,0},{32,16},{48,32},{64,48},{80,64},{96,80},{112,96},{128,112},... | collective-permute-start | bytes 98312 | tf_op jit(solution)/shard_map/ppermute | solution.py:19
  58.7 17.8 %collective-permute-start.6 = (f32[1,66,256]{2,1,0:T(8,128)S(1)}, f32[1,66,256]{2,1,0:T(8,128)S(1)}, u32[]{:S(2)}, u32[]{:S(2)}) collective-permute-start(f32[1,66,256]{2,1,0:T(8,128)S(1)} %get-tuple-element.10), channel_id=1, source_target_pairs={{0,1},{1,2},{2,3},{3,4},{4,5},{5,6},{6,7},{7,8},{8,9},{9,10},{10,1... | collective-permute-start | bytes 202760 | tf_op jit(solution)/shard_map/ppermute | solution.py:16
  61.7 15.6 %collective-permute-start.7 = (f32[1,66,256]{2,1,0:T(8,128)S(1)}, f32[1,66,256]{2,1,0:T(8,128)S(1)}, u32[]{:S(2)}, u32[]{:S(2)}) collective-permute-start(f32[1,66,256]{2,1,0:T(8,128)S(1)} %get-tuple-element.11), channel_id=1, source_target_pairs={{1,0},{2,1},{3,2},{4,3},{5,4},{6,5},{7,6},{8,7},{9,8},{10,9},{11,1... | collective-permute-start | bytes 202760 | tf_op jit(solution)/shard_map/ppermute | solution.py:19
  80.1 496.6 %copy-start = (f32[32,64,256]{2,1,0:T(8,128)}, f32[32,64,256]{2,1,0:T(8,128)S(1)}, u32[]{:S(2)}) copy-start(f32[32,64,256]{2,1,0:T(8,128)S(1)} %get-tuple-element.8) | copy-start | bytes 6291460
  80.1 495.0 %copy-start.1 = (f32[2,128,256]{2,1,0:T(8,128)S(1)}, f32[2,128,256]{2,1,0:T(8,128)}, u32[]{:S(2)}) copy-start(f32[2,128,256]{2,1,0:T(8,128)} %param.16) | copy-start | bytes 786436
  81.8 941.2 %all-reduce.5.cloned.1.call-start = ((), (), s32[]{:S(2)}) async-start(), calls=%async_computation.1 | async-start | bytes 262144 | tf_op jit(solution)/shard_map/psum | solution.py:107
Sparse Core Ops, SparseCore 0:
  82.0 467.8 all-reduce.2
  585.0 438.0 all-reduce.4
where the time goes:
time: 1060 us
  waiting for transfers between devices  910 us (86%)
  starting transfers between devices  57.2 us (5%)
  other arithmetic  56.7 us (5%)
  matrix products  21.4 us (2%)
  between operations  13.8 us (1%)
    psum x2, waiting for transfers between devices, body(): lax.psum(matmul_exact(((local_index[:, None] == cell_index[None, :]) & ow...  906 us
    ppermute x4, starting transfers between devices, extended(): lax.ppermute(lax.slice_in_dim(block, 0, width, axis=dim), axis, backward)  43.6 us
    another operation x6, other arithmetic, batch_weights(): factor = jnp.linalg.cholesky(system)  24.8 us
  transfers between devices with their start and end apart: 10, of which 6 were waited for; matrix products, arithmetic and copies ran while one was open for 1% of the time, Pallas kernels for 0%

commit v1 on v0

v1 whole, which is shorter than its diff:
```python
import functools
import jax
import jax.numpy as jnp
from jax import lax
from jax.experimental import pallas as pl
from jax.experimental.pallas import tpu as pltpu
from jax.sharding import PartitionSpec as P

BATCHES = 2
MESH = pl.DeviceIdType.MESH
PAD = 8
LANES = 128
HIGHEST = lax.Precision.HIGHEST
ONE_STEP = ((0, 0), (-1, 0), (1, 0), (0, -1), (0, 1))
TWO_STEPS = tuple(sorted({(a + c, b + d) for a, b in ONE_STEP for c, d in ONE_STEP}))


def split_mesh(lon_count, lat_count):
    plane_lat = 8 if lat_count == 16 else lat_count // 2
    line_lon = 8 if lon_count == 32 else lon_count // 2
    return lon_count // line_lon, line_lon, lat_count // plane_lat, plane_lat


def shifted(field, rows, lanes):
    if rows:
        field = pltpu.roll(field, rows % field.shape[0], 0)
    if lanes:
        field = pltpu.roll(field, lanes % field.shape[1], 1)
    return field


def link_weights(speed_lat, speed_lon, row, total_rows):
    inside = (row >= 0) & (row < total_rows)
    lat_plus = jnp.maximum(speed_lat, 0.0)
    lat_minus = jnp.minimum(speed_lat, 0.0)
    lon_plus = jnp.maximum(speed_lon, 0.0)
    lon_minus = jnp.minimum(speed_lon, 0.0)
    zero = jnp.zeros_like(speed_lat)
    return {
        (0, 0): jnp.where(inside, 1.0 - lat_plus + lat_minus - lon_plus + lon_minus, zero),
        (-1, 0): jnp.where(inside & (row > 0), lat_plus, zero),
        (1, 0): jnp.where(inside & (row < total_rows - 1), -lat_minus, zero),
        (0, -1): jnp.where(inside, lon_plus, zero),
        (0, 1): jnp.where(inside, -lon_minus, zero),
    }


def gather_kernel(
    sizes, state_ref, courant_ref, where_ref,
    priors_ref, field_ref,
    near_ns, near_ew, near_corner, reach, wide, stencil, links, weights, part, pieces, piece, line, got,
    grid, edge_send, edge_got,
    near_sem, reach_sem, part_sem, line_sem, all_sem, send_sem, out_sem,
):
    lon_count, lat_count = sizes
    plane_lon, line_lon, line_lat, plane_lat = split_mesh(lon_count, lat_count)
    plane, lines = plane_lon * plane_lat, line_lat * line_lon
    rows, cols, members = state_ref.shape
    total_rows, total_cols = rows * lat_count, cols * lon_count
    nobs = where_ref.shape[2]
    lon, lat = lax.axis_index("lon"), lax.axis_index("lat")
    plane_me = (lon // line_lon) * plane_lat + lat % plane_lat
    line_me = (lat // plane_lat) * line_lon + lon % line_lon

    def plane_device(index):
        return {
            "lon": (index // plane_lat) * line_lon + lon % line_lon,
            "lat": (lat // plane_lat) * plane_lat + index % plane_lat,
        }

    def line_device(index):
        return {
            "lon": (lon // line_lon) * line_lon + index % line_lon,
            "lat": (index // line_lon) * plane_lat + lat % plane_lat,
        }

    def neighbour(lat_step, lon_step):
        return {
            "lon": lax.rem(lon + lon_step + lon_count, lon_count),
            "lat": lax.rem(lat + lat_step + lat_count, lat_count),
        }

    around = [(a, b) for a in (-1, 0, 1) for b in (-1, 0, 1) if a or b]

    barrier = pltpu.get_barrier_semaphore()
    for step in around:
        pl.semaphore_signal(barrier, inc=1, device_id=neighbour(*step), device_id_type=MESH)

    def greet_line(d, carry):
        target = line_device(lax.rem(line_me + d, lines))
        pl.semaphore_signal(barrier, inc=1, device_id=target, device_id_type=MESH)
        return carry

    def greet_plane(d, carry):
        target = plane_device(lax.rem(plane_me + d, plane))
        pl.semaphore_signal(barrier, inc=1, device_id=target, device_id_type=MESH)
        return carry

    lax.fori_loop(1, lines, greet_line, 0)
    lax.fori_loop(1, plane, greet_plane, 0)

    for r in range(rows):
        grid[r + 2, PAD : PAD + cols, :] = state_ref[r].astype(jnp.float32)
    for side, first in ((0, 0), (1, cols - 2)):
        for j in range(2):
            edge_send[side, j] = state_ref[:, first + j, :].astype(jnp.float32)
    pl.semaphore_wait(barrier, len(around) + plane - 1 + lines - 1)

    copies = []

    def send(src, dst, sem, step):
        copy = pltpu.make_async_remote_copy(
            src_ref=src, dst_ref=dst, send_sem=sem.at[0], recv_sem=sem.at[1],
            device_id=neighbour(*step), device_id_type=MESH,
        )
        copy.start()
        copies.append(copy)
        return copy

    low, high = pl.ds(0, 8), pl.ds(rows - 8, 8)
    near = []
    for index, (a, b) in enumerate(around):
        source = courant_ref.at[:, {-1: low, 1: high}[a], :] if a else courant_ref
        if a and b:
            target = near_corner.at[(0 if a > 0 else 2) + (0 if b > 0 else 1)]
        elif a:
            target = near_ns.at[0 if a > 0 else 1]
        else:
            target = near_ew.at[0 if b > 0 else 1]
        near.append(send(source, target, near_sem.at[index], (a, b)))

    far = []
    inner = pl.ds(PAD, cols)
    blocks = {
        (1, 0): (grid.at[pl.ds(rows, 2), inner], grid.at[pl.ds(0, 2), inner]),
        (-1, 0): (grid.at[pl.ds(2, 2), inner], grid.at[pl.ds(rows + 2, 2), inner]),
        (0, 1): (edge_send.at[1], edge_got.at[0]),
        (0, -1): (edge_send.at[0], edge_got.at[1]),
        (1, 1): (grid.at[rows + 1, pl.ds(cols, 8)], grid.at[1, pl.ds(0, 8)]),
        (1, -1): (grid.at[rows + 1, pl.ds(PAD, 8)], grid.at[1, pl.ds(PAD + cols, 8)]),
        (-1, 1): (grid.at[2, pl.ds(cols, 8)], grid.at[rows + 2, pl.ds(0, 8)]),
        (-1, -1): (grid.at[2, pl.ds(PAD, 8)], grid.at[rows + 2, pl.ds(PAD + cols, 8)]),
    }
    for index, step in enumerate(around):
        far.append(send(*blocks[step], reach_sem.at[index], step))
    for copy in near:
        copy.wait_recv()

    lane = lax.broadcasted_iota(jnp.int32, (8, LANES), 1)

    def assemble(own, west, east):
        blank = jnp.zeros((8, LANES - cols), jnp.float32)
        own = jnp.concatenate([own, blank], axis=1)
        west = jnp.concatenate([blank, west], axis=1)
        east = jnp.concatenate([blank, east], axis=1) if cols * 2 == LANES else None
        return jnp.where(lane < cols, own, jnp.where(lane < cols + 2, east, west))

    for c in range(2):
        reach[c, 0:8] = assemble(near_ns[0, c], near_corner[0, c], near_corner[1, c])
        for r in range(0, rows, 8):
            band = pl.ds(r, 8)
            reach[c, r + 8 : r + 16] = assemble(courant_ref[c, band], near_ew[0, c, band], near_ew[1, c, band])
        reach[c, rows + 8 : rows + 16] = assemble(near_ns[1, c], near_corner[2, c], near_corner[3, c])

    row = lax.broadcasted_iota(jnp.int32, (rows + 16, LANES), 0) - 8 + lat * rows
    weight = link_weights(reach[0], reach[1], row, total_rows)

    arrived = {step: shifted(weight[step], *step) for step in ONE_STEP}
    sums = {}
    for first in ONE_STEP:
        for second in ONE_STEP:
            total = (first[0] + second[0], first[1] + second[1])
            term = shifted(arrived[first] * weight[second], *second)
            sums[total] = sums[total] + term if total in sums else term
    half = lax.broadcasted_iota(jnp.int32, (rows // 2, LANES), 1) < cols
    for index, total in enumerate(TWO_STEPS):
        wide[index] = sums[total][8 : 8 + rows]
        even = wide[index, pl.ds(0, rows // 2, 2), :]
        odd = wide[index, pl.ds(1, rows // 2, 2), :]
        stencil[index] = jnp.where(half, even, pltpu.roll(odd, cols, 1))

    cells = rows * cols
    flat_lane = lax.broadcasted_iota(jnp.int32, (nobs, LANES), 1)
    second_row = jnp.where(flat_lane >= cols, 1, 0)
    column = flat_lane - second_row * cols
    flat_state = state_ref[...].reshape(cells, members)
    for batch in range(BATCHES):
        where = jnp.concatenate([where_ref[batch], jnp.zeros((8 - 3, nobs), jnp.int32)], axis=0)
        where = jnp.transpose(where.astype(jnp.float32)).astype(jnp.int32)
        obs_row = where[:, 0:1] - lat * rows
        obs_col = where[:, 1:2] - lon * cols + 2
        obs_col = jnp.where(obs_col < 0, obs_col + total_cols, obs_col) - 2
        obs_col = jnp.where(obs_col >= total_cols - 2, obs_col - total_cols, obs_col)
        lon_step = column - obs_col
        lat_base = second_row - obs_row

        def one_pair(pair, carry):
            lat_step = lat_base + 2 * pair
            total = jnp.zeros((nobs, LANES), jnp.float32)
            for a in range(-2, 3):
                for b in range(-2, 3):
                    if (a, b) in TWO_STEPS:
                        value = stencil[TWO_STEPS.index((a, b)), pl.ds(pair, 1), :]
                        total = jnp.where((lat_step == a) & (lon_step == b), value, total)
            upper = total.astype(jnp.bfloat16)
            columns = pl.ds(pl.multiple_of(pair * LANES, LANES), LANES)
            weights[0:nobs, columns] = upper
            weights[nobs : 2 * nobs, columns] = (total - upper.astype(jnp.float32)).astype(jnp.bfloat16)
            return carry

        lax.fori_loop(0, rows // 2, one_pair, 0)
        share = jnp.dot(weights[...], flat_state, preferred_element_type=jnp.float32)
        part[batch] = share[:nobs] + share[nobs:]

        def send_part(d, carry):
            index = lax.rem(plane_me + d, plane)
            copy = pltpu.make_async_remote_copy(
                src_ref=part.at[batch, *tile_of(index)], dst_ref=pieces.at[batch, d],
                send_sem=send_sem.at[batch, 0], recv_sem=part_sem.at[batch],
                device_id=plane_device(index), device_id_type=MESH,
            )
            copy.start()
            return carry

        def tile_of(index):
            halves = members // LANES
            band = nobs * halves // plane
            return (
                pl.ds(pl.multiple_of((index // halves) * band, band), band),
                pl.ds(pl.multiple_of((index % halves) * LANES, LANES), LANES),
            )

        lax.fori_loop(1, plane, send_part, 0)

    for batch in range(BATCHES):
        pltpu.make_async_copy(pieces.at[batch, 1:plane], pieces.at[batch, 1:plane], part_sem.at[batch]).wait()
        piece[batch] = part[batch, *tile_of(plane_me)] + jnp.sum(pieces[batch, 1:plane], axis=0)

        def send_line(d, carry):
            copy = pltpu.make_async_remote_copy(
                src_ref=piece.at[batch], dst_ref=line.at[batch, d],
                send_sem=send_sem.at[batch, 1], recv_sem=line_sem.at[batch],
                device_id=line_device(lax.rem(line_me + d, lines)), device_id_type=MESH,
            )
            copy.start()
            return carry

        lax.fori_loop(1, lines, send_line, 0)

    for copy in far:
        copy.wait_recv()
    for side, first in ((0, PAD - 2), (1, PAD + cols)):
        for j in range(2):
            grid[2 : 2 + rows, first + j, :] = edge_got[side, j]
    width = cols + 2 * PAD
    for index, step in enumerate(ONE_STEP):
        upright = jnp.concatenate([weight[step], jnp.zeros((LANES - rows - 16, LANES), jnp.float32)], axis=0)
        links[index] = jnp.transpose(pltpu.roll(upright, PAD, 1))[:width]

    def one_row(r, source, target):
        rolled = [
            jnp.broadcast_to(pltpu.roll(links[i], lax.rem(LANES - r - 6, LANES), 1)[:, 0:1], (width, LANES))
            for i in range(len(ONE_STEP))
        ]
        for first in range(0, members, LANES):
            lanes = pl.ds(first, LANES)
            here = source[r, :, lanes]
            target(
                r, lanes,
                rolled[0] * here
                + rolled[1] * source[r - 1, :, lanes]
                + rolled[2] * source[r + 1, :, lanes]
                + rolled[3] * pltpu.roll(here, 1, 0)
                + rolled[4] * pltpu.roll(here, width - 1, 0),
            )

    def first_row(r, carry):
        def store(r, lanes, value):
            halfway[r, :, lanes] = value

        one_row(r, grid, store)
        return carry

    halfway = got[1]
    lax.fori_loop(1, rows + 3, first_row, 0)

    def second_row_of(r, carry):
        def store(r, lanes, value):
            grid[r, :, lanes] = value

        one_row(r, halfway, store)
        return carry

    for copy in far:
        copy.wait_send()
    lax.fori_loop(2, rows + 2, second_row_of, 0)
    out = pltpu.make_async_copy(grid.at[pl.ds(2, rows), pl.ds(PAD, cols)], field_ref, out_sem)
    out.start()

    priors = got[0]
    for batch in range(BATCHES):
        pltpu.make_async_copy(line.at[batch, 1:lines], line.at[batch, 1:lines], line_sem.at[batch]).wait()
        mine = tile_of(plane_me)
        priors[batch, *mine] = piece[batch] + jnp.sum(line[batch, 1:lines], axis=0)

        def send_all(d, carry):
            copy = pltpu.make_async_remote_copy(
                src_ref=priors.at[batch, *mine], dst_ref=priors.at[batch, *mine],
                send_sem=send_sem.at[batch, 2], recv_sem=all_sem.at[batch],
                device_id=plane_device(lax.rem(plane_me + d, plane)), device_id_type=MESH,
            )
            copy.start()
            return carry

        lax.fori_loop(1, plane, send_all, 0)
    for batch in range(BATCHES):
        block = pieces.at[batch, 1:plane]
        pltpu.make_async_copy(block, block, all_sem.at[batch]).wait()
        priors_ref[batch] = priors[batch]

    for copy in near:
        copy.wait_send()
    for batch in range(BATCHES):
        block = pieces.at[batch, 1:plane]
        pltpu.make_async_copy(block, block, send_sem.at[batch, 0]).wait()
        block = line.at[batch, 1:lines]
        pltpu.make_async_copy(block, block, send_sem.at[batch, 1]).wait()
        block = pieces.at[batch, 1:plane]
        pltpu.make_async_copy(block, block, send_sem.at[batch, 2]).wait()
    out.wait()


def gather(state, courant, where, lon_count, lat_count):
    rows, cols, members = state.shape
    nobs = where.shape[2]
    plane_lon, line_lon, line_lat, plane_lat = split_mesh(lon_count, lat_count)
    plane, lines = plane_lon * plane_lat, line_lat * line_lon
    band = nobs * (members // LANES) // plane
    width = cols + 2 * PAD
    f32 = jnp.float32
    vmem = pl.BlockSpec(memory_space=pltpu.VMEM)
    dma = pltpu.SemaphoreType.DMA
    return pl.pallas_call(
        functools.partial(gather_kernel, (lon_count, lat_count)),
        out_shape=(
            jax.ShapeDtypeStruct((BATCHES, nobs, members), f32),
            jax.ShapeDtypeStruct((rows, cols, members), f32),
        ),
        in_specs=[vmem] * 3,
        out_specs=(vmem, pl.BlockSpec(memory_space=pl.ANY)),
        scratch_shapes=[
            pltpu.VMEM((2, 2, 8, cols), f32),
            pltpu.VMEM((2, 2, rows, cols), f32),
            pltpu.VMEM((4, 2, 8, cols), f32),
            pltpu.VMEM((2, rows + 16, LANES), f32),
            pltpu.VMEM((len(TWO_STEPS), rows, LANES), f32),
            pltpu.VMEM((len(TWO_STEPS), rows // 2, LANES), f32),
            pltpu.VMEM((len(ONE_STEP), width, LANES), f32),
            pltpu.VMEM((2 * nobs, rows * cols), jnp.bfloat16),
            pltpu.VMEM((BATCHES, nobs, members), f32),
            pltpu.VMEM((BATCHES, plane, band, LANES), f32),
            pltpu.VMEM((BATCHES, band, LANES), f32),
            pltpu.VMEM((BATCHES, lines, band, LANES), f32),
            [pltpu.VMEM((BATCHES, nobs, members), f32), pltpu.VMEM((rows + 4, width, members), f32)],
            pltpu.VMEM((rows + 4, width, members), f32),
            pltpu.VMEM((2, 2, rows, members), f32),
            pltpu.VMEM((2, 2, rows, members), f32),
            dma((8, 2)),
            dma((8, 2)),
            dma((BATCHES,)),
            dma((BATCHES,)),
            dma((BATCHES,)),
            dma((BATCHES, 3)),
            dma,
        ],
        compiler_params=pltpu.CompilerParams(
            collective_id=0, has_side_effects=True, vmem_limit_bytes=48 * 1024 * 1024
        ),
        name="advance_and_gather",
    )(state, courant, where)


def matmul_exact(left, right):
    return jnp.dot(left, right, precision=HIGHEST, preferred_element_type=jnp.float32)


def taper_weights(cell_lat, cell_lon, obs_lat, obs_lon, radius, width):
    lat_gap = cell_lat - obs_lat
    lon_gap = jnp.abs(cell_lon - obs_lon)
    lon_gap = jnp.minimum(lon_gap, width - lon_gap)
    distance_sq = (lat_gap * lat_gap + lon_gap * lon_gap).astype(jnp.float32)
    radius_sq = (radius * radius).astype(jnp.float32)
    return jnp.square(jnp.maximum(1.0 - distance_sq / radius_sq, 0.0))


def batch_weights(priors, values, variance, noise):
    members = priors.shape[1]
    anomaly = priors - jnp.mean(priors, axis=1, keepdims=True)
    system = matmul_exact(anomaly, anomaly.T) / (members - 1) + jnp.diag(variance)
    misfit = values[:, None] + jnp.sqrt(variance)[:, None] * noise - priors
    factor = jnp.linalg.cholesky(system)
    halfway = lax.linalg.triangular_solve(factor, misfit, left_side=True, lower=True)
    weights = lax.linalg.triangular_solve(
        factor, halfway, left_side=True, lower=True, transpose_a=True
    )
    return (anomaly, weights)


def body(ensemble_state, courant, obs_where, obs_value, obs_variance, obs_noise):
    rows_tile, cols_tile, members = ensemble_state.shape
    lat_count, lon_count = lax.axis_size("lat"), lax.axis_size("lon")
    total_cols = cols_tile * lon_count
    row_start = lax.axis_index("lat") * rows_tile
    col_start = lax.axis_index("lon") * cols_tile
    priors, field = gather(ensemble_state, courant, obs_where, lon_count, lat_count)
    ensemble = field.reshape(rows_tile * cols_tile, members)
    cell_index = jnp.arange(rows_tile * cols_tile, dtype=jnp.int32)
    cell_lat = (row_start + cell_index // cols_tile)[:, None]
    cell_lon = (col_start + cell_index % cols_tile)[:, None]

    def update(cells, lat, lon, batch, anomaly_obs, weights):
        taper = taper_weights(
            lat, lon,
            obs_where[batch, 0][None, :], obs_where[batch, 1][None, :], obs_where[batch, 2][None, :],
            total_cols,
        )
        anomaly = cells - jnp.mean(cells, axis=1, keepdims=True)
        covariance = matmul_exact(anomaly, anomaly_obs.T) / (members - 1)
        return cells + matmul_exact(taper * covariance, weights)

    for batch in range(BATCHES):
        anomaly_obs, weights = batch_weights(
            priors[batch], obs_value[batch], obs_variance[batch], obs_noise[batch]
        )
        ensemble = update(ensemble, cell_lat, cell_lon, batch, anomaly_obs, weights)
        if batch + 1 < BATCHES:
            later = update(
                priors[batch + 1],
                obs_where[batch + 1, 0][:, None], obs_where[batch + 1, 1][:, None],
                batch, anomaly_obs, weights,
            )
            priors = priors.at[batch + 1].set(later)
    return ensemble.reshape(rows_tile, cols_tile, members).astype(jnp.bfloat16)


def solution(mesh):
    placed = (P("lat", "lon", None), P(None, "lat", "lon"), P(), P(), P(), P())
    return jax.shard_map(
        body, mesh=mesh, in_specs=placed, out_specs=P("lat", "lon", None), check_vma=False
    )
```

time: 1060 us -> 136 us (0.13)
  waiting for transfers between devices: 910 us -> 0 us
  Pallas kernels: 0 us -> 63.7 us
  starting transfers between devices: 57.2 us -> 0 us
  between operations: 13.8 us -> 0.39 us
    psum x2 -> x0, waiting for transfers between devices: 906 us -> none  [body(): lax.psum(matmul_exact(((local_index[:, None] == cell_index[None, :]) & ow...]
    pallas_call x0 -> x1, Pallas kernels: none -> 63.7 us  [gather(): pl.pallas_call(functools.partial(gather_kernel, (lon_count, lat_count)),...]
    ppermute x8 -> x0, starting transfers between devices: 57 us -> none  [the longest x4 43.6 us: extended(): lax.ppermute(lax.slice_in_dim(block, 0, width, axis=dim), axis, backward)]
  transfers between devices with their start and end apart: 10 -> 0, of which waited for: 6 -> 0; matrix products, arithmetic and copies ran while one was open for 1% -> 0% of each run, Pallas kernels for 0% -> 0%
where the time goes in v1:
time: 136 us; the launch traced here: 135 us
  Pallas kernels  63.7 us (47%)
  other arithmetic  50.6 us (37%)
  matrix products  15.5 us (11%)
  local copies, waits for them, and re-layouts  5.01 us (4%)
    pallas_call x1, Pallas kernels, gather(): pl.pallas_call(functools.partial(gather_kernel, (lon_count, lat_count)),...  63.7 us
    another operation x6, other arithmetic, batch_weights(): factor = jnp.linalg.cholesky(system)  25.8 us
    another operation x4, other arithmetic, batch_weights(): lax.linalg.triangular_solve(factor, halfway, left_side=True, lower=True,...  20.9 us
    dot_general x8, matrix products, matmul_exact(): jnp.dot(left, right, precision=HIGHEST, preferred_element_type=jnp.float32)  13.3 us
    unnamed x39, local copies, waits for them, and re-layouts  2.74 us

profile of v1, /device:TPU:1, one launch (start us, length us, event | category | flops | bytes accessed | tf_op | source)
XLA Modules:
  0.0 135.2 jit_solution(16897167157819643075)
XLA Ops:
  0.0 0.7 copy.7.where_ref
  0.7 1.2 copy-done
  1.9 0.8 copy-done.1
  2.7 63.7 %advance_and_gather.1 = (f32[2,128,256]{2,1,0:T(8,128)S(1)}, f32[32,64,256]{2,1,0:T(8,128)S(1)}) custom-call(bf16[32,64,256]{2,1,0:T(8,128)(2,1)S(1)} %copy-done, f32[2,32,64]{2,1,0:T(8,128)S(1)} %copy-done.1, s32[2,3,128]{2,1,0:T(4,128)S(1)} %copy.7.where_ref), custom_call_target="tpu_custom_call" | custom-call | tf_op jit(solution)/shard_map/advance_and_gather/pallas_call | solution.py:343
  66.4 0.3 reduce_sum.45
  66.7 0.0 copy-start.4
  66.7 1.7 %broadcast_subtract_fusion = f32[32,64,256]{2,1,0:T(8,128)} fusion(f32[32,64,256]{2,1,0:T(8,128)S(1)} %get-tuple-element.22, f32[32,64]{1,0:T(8,128)S(1)} %broadcast_multiply_fusion), kind=kLoop, calls=%fused_computation.32 | loop fusion | flops 524288 | bytes 4202496 | tf_op jit(solution)/shard_map/sub | solution.py:427
  68.4 0.0 copy-done.4
  68.4 0.6 slice_bitcast_fusion.3
  69.0 0.1 slice_reduce_fusion
  69.1 0.5 broadcast_multiply_fusion.3
  69.6 3.6 %fusion.2 = f32[2048,128]{1,0:T(8,128)S(1)} fusion(f32[2048,256]{1,0:T(8,128)} %bitcast.92, f32[128]{0:T(128)S(1)} %get-tuple-element.27, s32[128]{0:T(128)S(1)} %get-tuple-element.28, s32[2048]{0:T(1024)S(1)} %get-tuple-element.45, s32[128]{0:T(128)S(1)} %get-tuple-element.29, s32[2048]{0:T(1024)S(1)} %get-tuple-element.44, ...), kind=kOutput, calls=%fused_computation.6 | convolution fusion | flops 809271296 | bytes 3295232 | tf_op jit(solution)/shard_map/dot_general | solution.py:384
  73.3 0.0 copy-done.12
  73.3 0.0 copy-done.14
  73.3 0.0 copy-done.16
  73.3 0.0 copy-done.5
  73.3 0.6 slice_bitcast_fusion.1
  73.9 0.0 copy-done.7
  73.9 0.3 fusion.4
  74.2 0.1 copy.9
  74.3 0.6 fusion.62
  75.0 12.5 %cholesky.44 = f32[128,128]{1,0:T(8,128)S(1)} custom-call(f32[128,128]{1,0:T(8,128)} %fusion.62), custom_call_target="Cholesky" | custom-call | tf_op jit(solution)/shard_map/jit(cholesky)/cholesky | solution.py:401
  87.6 0.6 compare_reduce_fusion.1
  88.2 0.7 fusion.46
  88.9 9.8 %custom-call.11 = f32[1,128,128]{1,2,0:T(8,128)S(1)} custom-call(f32[1,128,128]{2,1,0:T(8,128)S(1)} %fusion.46), custom_call_target="InvertDiagBlocksLowerTriangular" | custom-call | tf_op jit(solution)/shard_map/triangular_solve/custom-call.2 | solution.py:403
  98.7 0.8 fusion.83
  99.5 0.8 slice_bitcast_fusion
  100.2 1.3 fusion.27
  101.5 0.3 fusion.60
  101.8 0.0 copy-start.8
  101.8 0.0 copy-start.9
  101.8 1.9 %fusion.84 = (f32[2048]{0:T(1024)S(1)}, f32[2048,256]{1,0:T(8,128)S(1)}) fusion(f32[2048,256]{1,0:T(8,128)S(1)} %bitcast.91, f32[2048,128]{1,0:T(8,128)S(1)} %fusion.2, f32[128,256]{1,0:T(8,128)S(1)} %fusion.60), kind=kOutput, calls=%fused_computation.129 | convolution fusion | flops 806352896 | bytes 5382144 | tf_op jit(solution)/shard_map/dot_general | solution.py:384
  103.8 0.4 fusion.5
  104.2 0.4 fusion.85
  104.6 0.0 copy-start.3
  104.6 2.0 %fusion.1 = f32[2048,128]{1,0:T(8,128)S(1)} fusion(f32[2048,256]{1,0:T(8,128)S(1)} %get-tuple-element.39, f32[2048]{0:T(1024)S(1)} %broadcast_multiply_fusion.1, f32[128]{0:T(128)S(1)} %copy-done.10, s32[128]{0:T(128)S(1)} %copy-done.11, s32[128]{0:T(128)S(1)} %copy-done.9, s32[2048]{0:T(1024)S(1)} %get-tuple-element.45, s32[2048]{0:T(1024)S(1)} %get-tuple-element.44, ...), kind=kOutput, calls=%fused_computation.4 | convolution fusion | flops 809795584 | bytes 3303424 | tf_op jit(solution)/shard_map/dot_general | solution.py:384
  106.7 0.0 copy-done.2
  106.7 0.0 copy-done.6
  106.7 0.3 fusion.6
  107.0 0.1 copy.11
  107.1 11.9 %cholesky.55 = f32[128,128]{1,0:T(8,128)S(1)} custom-call(f32[128,128]{1,0:T(8,128)S(1)} %fusion.58), custom_call_target="Cholesky" | custom-call | tf_op jit(solution)/shard_map/jit(cholesky)/cholesky | solution.py:401
  119.1 0.6 compare_reduce_fusion
  119.7 0.7 fusion.47
  120.4 9.8 %custom-call.13 = f32[1,128,128]{1,2,0:T(8,128)S(1)} custom-call(f32[1,128,128]{2,1,0:T(8,128)S(1)} %fusion.47), custom_call_target="InvertDiagBlocksLowerTriangular" | custom-call | tf_op jit(solution)/shard_map/triangular_solve/custom-call.2 | solution.py:403
  130.2 0.0 copy-done.3
  130.2 0.4 fusion.24
  130.6 0.3 fusion.56
  130.9 4.3 %fusion = bf16[2048,256]{1,0:T(8,128)(2,1)} fusion(f32[2048,256]{1,0:T(8,128)} %copy-done.2, f32[2048,128]{1,0:T(8,128)S(1)} %fusion.1, f32[128,256]{1,0:T(8,128)S(1)} %fusion.56), kind=kOutput, calls=%fused_computation.2 | convolution fusion | flops 806354944 | bytes 4325376 | tf_op jit(solution)/shard_map/dot_general | solution.py:384
  (30 shorter events, 0.1 us)
Async XLA Ops:
  0.7 1.2 copy-start
  1.9 0.8 copy-start.1
  66.7 1.7 %copy-start.4 = (s32[2,3,128]{2,0,1:T(2,128)S(1)}, s32[2,3,128]{2,0,1:T(2,128)}, u32[]{:S(2)}) copy-start(s32[2,3,128]{2,0,1:T(2,128)} %param.15) | copy-start | bytes 9220
  69.0 4.3 %copy-start.12 = (f32[128]{0:T(128)}, f32[128]{0:T(128)S(1)}, u32[]{:S(2)}) copy-start(f32[128]{0:T(128)S(1)} %get-tuple-element.27) | copy-start | bytes 1540
  69.0 4.3 %copy-start.14 = (s32[128]{0:T(128)}, s32[128]{0:T(128)S(1)}, u32[]{:S(2)}) copy-start(s32[128]{0:T(128)S(1)} %get-tuple-element.28) | copy-start | bytes 1540
  69.0 4.3 %copy-start.16 = (s32[128]{0:T(128)}, s32[128]{0:T(128)S(1)}, u32[]{:S(2)}) copy-start(s32[128]{0:T(128)S(1)} %get-tuple-element.29) | copy-start | bytes 1540
  69.6 4.2 %copy-start.7 = (f32[128]{0:T(128)}, f32[128]{0:T(128)S(1)}, u32[]{:S(2)}) copy-start(f32[128]{0:T(128)S(1)} %get-tuple-element.43) | copy-start | bytes 1540
  69.6 3.7 %copy-start.5 = (f32[2,128]{1,0:T(2,128)S(1)}, f32[2,128]{1,0:T(2,128)}, u32[]{:S(2)}) copy-start(f32[2,128]{1,0:T(2,128)} %param.17) | copy-start | bytes 3076
  101.8 2.0 %copy-start.8 = (f32[128]{0:T(128)S(1)}, f32[128]{0:T(128)}, u32[]{:S(2)}) copy-start(f32[128]{0:T(128)} %copy-done.7) | copy-start | bytes 1540
  101.8 2.0 %copy-start.9 = (s32[128]{0:T(128)S(1)}, s32[128]{0:T(128)}, u32[]{:S(2)}) copy-start(s32[128]{0:T(128)} %get-tuple-element.26) | copy-start | bytes 1540
  101.8 2.0 %copy-start.11 = (s32[128]{0:T(128)S(1)}, s32[128]{0:T(128)}, u32[]{:S(2)}) copy-start(s32[128]{0:T(128)} %get-tuple-element.31) | copy-start | bytes 1540
  101.8 2.0 %copy-start.13 = (f32[128]{0:T(128)S(1)}, f32[128]{0:T(128)}, u32[]{:S(2)}) copy-start(f32[128]{0:T(128)} %copy-done.12) | copy-start | bytes 1540
  101.8 2.0 %copy-start.15 = (s32[128]{0:T(128)S(1)}, s32[128]{0:T(128)}, u32[]{:S(2)}) copy-start(s32[128]{0:T(128)} %copy-done.14) | copy-start | bytes 1540
  101.8 2.0 %copy-start.17 = (s32[128]{0:T(128)S(1)}, s32[128]{0:T(128)}, u32[]{:S(2)}) copy-start(s32[128]{0:T(128)} %copy-done.16) | copy-start | bytes 1540
  101.8 2.0 %copy-start.18 = (f32[128]{0:T(128)S(1)}, f32[128]{0:T(128)}, u32[]{:S(2)}) copy-start(f32[128]{0:T(128)} %get-tuple-element.42) | copy-start | bytes 1540
  101.8 2.8 %copy-start.10 = (f32[128]{0:T(128)S(1)}, f32[128]{0:T(128)}, u32[]{:S(2)}) copy-start(f32[128]{0:T(128)} %get-tuple-element.30) | copy-start | bytes 1540
  103.8 2.9 %copy-start.2 = (f32[2048,256]{1,0:T(8,128)}, f32[2048,256]{1,0:T(8,128)S(1)}, u32[]{:S(2)}) copy-start(f32[2048,256]{1,0:T(8,128)S(1)} %get-tuple-element.39) | copy-start | bytes 6291460
  104.6 2.1 %copy-start.6 = (f32[128]{0:T(128)S(1)}, f32[128]{0:T(128)}, u32[]{:S(2)}) copy-start(f32[128]{0:T(128)} %get-tuple-element.36) | copy-start | bytes 1540
  104.6 25.6 %copy-start.3 = (f32[2,128,256]{2,1,0:T(8,128)S(1)}, f32[2,128,256]{2,1,0:T(8,128)}, u32[]{:S(2)}) copy-start(f32[2,128,256]{2,1,0:T(8,128)} %param.18) | copy-start | bytes 786436

commit v2 on v1

--- a/solution.py
+++ b/solution.py
@@ -380,67 +380,223 @@
     )(state, courant, where)
 
 
-def matmul_exact(left, right):
-    return jnp.dot(left, right, precision=HIGHEST, preferred_element_type=jnp.float32)
-
-
-def taper_weights(cell_lat, cell_lon, obs_lat, obs_lon, radius, width):
-    lat_gap = cell_lat - obs_lat
-    lon_gap = jnp.abs(cell_lon - obs_lon)
-    lon_gap = jnp.minimum(lon_gap, width - lon_gap)
-    distance_sq = (lat_gap * lat_gap + lon_gap * lon_gap).astype(jnp.float32)
-    radius_sq = (radius * radius).astype(jnp.float32)
-    return jnp.square(jnp.maximum(1.0 - distance_sq / radius_sq, 0.0))
-
-
-def batch_weights(priors, values, variance, noise):
-    members = priors.shape[1]
-    anomaly = priors - jnp.mean(priors, axis=1, keepdims=True)
-    system = matmul_exact(anomaly, anomaly.T) / (members - 1) + jnp.diag(variance)
-    misfit = values[:, None] + jnp.sqrt(variance)[:, None] * noise - priors
-    factor = jnp.linalg.cholesky(system)
-    halfway = lax.linalg.triangular_solve(factor, misfit, left_side=True, lower=True)
-    weights = lax.linalg.triangular_solve(
-        factor, halfway, left_side=True, lower=True, transpose_a=True
+def matmul_exact(left, right, contract=(1, 0)):
+    return lax.dot_general(
+        left, right, (((contract[0],), (contract[1],)), ((), ())),
+        precision=HIGHEST, preferred_element_type=jnp.float32,
     )
-    return (anomaly, weights)
+
+
+def halves_of(value):
+    upper = value.astype(jnp.bfloat16)
+    return upper, (value - upper.astype(jnp.float32)).astype(jnp.bfloat16)
+
+
+def matmul_halves(left, right):
+    total = jnp.dot(left[0], right[1], preferred_element_type=jnp.float32)
+    total += jnp.dot(left[1], right[0], preferred_element_type=jnp.float32)
+    return total + jnp.dot(left[0], right[0], preferred_element_type=jnp.float32)
+
+
+def solve_pivot(pivot, rows):
+    count = len(rows)
+    pivot, rows, factor, inverse = dict(pivot), list(rows), {}, {}
+    for j in range(0, count, 2):
+        a, b, c = pivot[j, j], pivot[j + 1, j], pivot[j + 1, j + 1]
+        scale = 1.0 / (a * c - b * b)
+        inverse[j] = first, cross, last = c * scale, -b * scale, a * scale
+        for i in range(j + 2, count):
+            factor[i, j] = pivot[i, j] * first + pivot[i, j + 1] * cross
+            factor[i, j + 1] = pivot[i, j] * cross + pivot[i, j + 1] * last
+        for i in range(j + 2, count):
+            for k in range(j + 2, i + 1):
+                pivot[i, k] -= factor[i, j] * pivot[k, j] + factor[i, j + 1] * pivot[k, j + 1]
+    for j in range(0, count, 2):
+        for i in range(j + 2, count):
+            rows[i] -= factor[i, j] * rows[j] + factor[i, j + 1] * rows[j + 1]
+    for j in range(0, count, 2):
+        first, cross, last = inverse[j]
+        rows[j], rows[j + 1] = first * rows[j] + cross * rows[j + 1], cross * rows[j] + last * rows[j + 1]
+    for i in reversed(range(0, count, 2)):
+        for j in range(i):
+            rows[j] -= factor[i, j] * rows[i] + factor[i + 1, j] * rows[i + 1]
+    return rows
+
+
+def tree_sum(terms):
+    while len(terms) > 1:
+        terms = [a + b for a, b in zip(terms[::2], terms[1::2])] + terms[len(terms) // 2 * 2 :]
+    return terms[0]
+
+
+def inverse_of(system, panel=32):
+    size = system.shape[0]
+    spread = (8, size)
+    lane = lax.broadcasted_iota(jnp.int32, spread, 1)
+    sub = lax.broadcasted_iota(jnp.int32, spread, 0)
+    panel_lane = lax.broadcasted_iota(jnp.int32, (panel, size), 1)
+    panel_sub = lax.broadcasted_iota(jnp.int32, (panel, size), 0)
+    whole_lane = lax.broadcasted_iota(jnp.int32, (size, size), 1)
+    for start in range(0, size, panel):
+        old = system[start : start + panel]
+        bands = [old[i : i + 8] for i in range(0, panel, 8)]
+        for here in range(panel // 8):
+            first = start + 8 * here
+            inside = (lane >= first) & (lane < first + 8)
+            columns = [
+                [jnp.broadcast_to(band[:, first + j : first + j + 1], spread) for j in range(8)] for band in bands
+            ]
+            pivot = {
+                (i, j): jnp.broadcast_to(columns[here][j][i : i + 1], spread) for i in range(8) for j in range(i + 1)
+            }
+            rows = [
+                jnp.where(inside, jnp.where(lane == first + j, -1.0, 0.0), jnp.broadcast_to(bands[here][j : j + 1], spread))
+                for j in range(8)
+            ]
+            rows = solve_pivot(pivot, rows)
+            for i, band in enumerate(bands):
+                if i != here:
+                    terms = [columns[i][j] * rows[j] for j in range(8)]
+                    bands[i] = jnp.where(inside, 0.0, band) - tree_sum(terms)
+            swept = rows[7]
+            for j in range(7):
+                swept = jnp.where(sub == j, rows[j], swept)
+            bands[here] = swept
+        swept = jnp.concatenate(bands, axis=0)
+        inside = (panel_lane >= start) & (panel_lane < start + panel)
+        old = jnp.where(inside, jnp.where(panel_lane == panel_sub + start, -1.0, 0.0), old)
+        inside = (whole_lane >= start) & (whole_lane < start + panel)
+        system = jnp.where(inside, 0.0, system) - matmul_exact(old, swept, (0, 0))
+        parts = [system[:start], swept, system[start + panel :]]
+        system = jnp.concatenate([part for part in parts if part.shape[0]], axis=0)
+    return -system
+
+
+def square(value):
+    return value * value
+
+
+def analysis_kernel(
+    sizes, priors_ref, field_ref, where_ref, value_ref, variance_ref, noise_ref, out_ref,
+    field, spread, analysis, field_sem, out_sem,
+):
+    lon_count, lat_count = sizes
+    rows, cols, members = field_ref.shape
+    nobs = where_ref.shape[2]
+    total_cols = cols * lon_count
+    first_row, first_col = lax.axis_index("lat") * rows, lax.axis_index("lon") * cols
+    fetch = pltpu.make_async_copy(field_ref, field, field_sem)
+    fetch.start()
+
+    blank = jnp.zeros((8 - 2 * BATCHES, nobs), jnp.float32)
+    upright = jnp.transpose(jnp.concatenate([value_ref[...], variance_ref[...], blank], axis=0))
+    eye = lax.broadcasted_iota(jnp.int32, (nobs, nobs), 0) == lax.broadcasted_iota(jnp.int32, (nobs, nobs), 1)
+
+    def lon_distance(cell, obs):
+        gap = jnp.abs(cell - obs)
+        return jnp.minimum(gap, total_cols - gap)
+
+    def scaled_square(gap, radius):
+        return square(gap).astype(jnp.float32) / square(radius).astype(jnp.float32)
+
+    def weights_of(batch, priors, anomaly):
+        variance = upright[:, BATCHES + batch : BATCHES + batch + 1]
+        system = matmul_exact(anomaly, anomaly, (1, 1)) / (members - 1)
+        system += jnp.where(eye, variance, 0.0)
+        misfit = upright[:, batch : batch + 1] + jnp.sqrt(variance) * noise_ref[batch] - priors
+        return matmul_exact(inverse_of(system), misfit)
+
+    def centred(priors):
+        return priors - jnp.mean(priors, axis=1, keepdims=True)
+
+    obs = [[where_ref[batch, i : i + 1, :] for i in range(3)] for batch in range(BATCHES)]
+    priors = [priors_ref[batch] for batch in range(BATCHES)]
+    anomaly, weights = [centred(priors[0])], []
+    weights.append(weights_of(0, priors[0], anomaly[0]))
+
+    where = jnp.concatenate([where_ref[1].astype(jnp.float32), jnp.zeros((8 - 3, nobs), jnp.float32)], axis=0)
+    where = jnp.transpose(where).astype(jnp.int32)
+    lat_gap = where[:, 0:1] - obs[0][0]
+    lon_gap = lon_distance(where[:, 1:2], obs[0][1])
+    distance = (square(lat_gap) + square(lon_gap)).astype(jnp.float32)
+    taper = square(jnp.maximum(1.0 - distance / square(obs[0][2]).astype(jnp.float32), 0.0))
+    covariance = matmul_exact(centred(priors[1]), anomaly[0], (1, 1)) / (members - 1)
+    priors[1] += matmul_exact(taper * covariance, weights[0])
+    anomaly.append(centred(priors[1]))
+    carried = halves_of(matmul_exact(centred(weights[0]), anomaly[1], (1, 1)) / (members - 1))
+
+    both = [jnp.transpose(part) for part in halves_of(jnp.concatenate(anomaly, axis=0) / (members - 1))]
+    cell_lon = first_col + lax.broadcasted_iota(jnp.int32, (cols, 1), 0)
+    lon_part = [scaled_square(lon_distance(cell_lon, lon), radius) for _, lon, radius in obs]
+    chunk = 4
+    fetch.wait()
+
+    def taper_of(batch, row):
+        lat, _, radius = obs[batch]
+        room = 1.0 - scaled_square(first_row + row - lat, radius)
+        return square(jnp.maximum(room - lon_part[batch], 0.0))
+
+    def spread_chunk(index, carry):
+        cells = field[pl.ds(index * chunk, chunk)].reshape(chunk * cols, members)
+        covariance = matmul_halves(halves_of(cells), both)
+        tapers = [
+            jnp.concatenate([taper_of(batch, index * chunk + r) for r in range(chunk)], axis=0)
+            for batch in range(BATCHES)
+        ]
+        first = tapers[0] * covariance[:, :nobs]
+        second = tapers[1] * (covariance[:, nobs:] + matmul_halves(halves_of(first), carried))
+        at = pl.ds(pl.multiple_of(index * chunk * cols, chunk * cols), chunk * cols)
+        for i, part in enumerate(halves_of(jnp.concatenate([first, second], axis=1))):
+            spread[i, at] = part
+        return carry
+
+    lax.fori_loop(0, rows // chunk, spread_chunk, 0)
+
+    weights.append(weights_of(1, priors[1], anomaly[1]))
+    both_weights = halves_of(jnp.concatenate(weights, axis=0))
+
+    def copy_out(index):
+        at = pl.ds(index * chunk, chunk)
+        return pltpu.make_async_copy(analysis.at[at], out_ref.at[at], out_sem.at[index])
+
+    def update_chunk(index, carry):
+        at = pl.ds(pl.multiple_of(index * chunk * cols, chunk * cols), chunk * cols)
+        change = matmul_halves((spread[0, at], spread[1, at]), both_weights)
+        at = pl.ds(index * chunk, chunk)
+        analysis[at] = (field[at] + change.reshape(chunk, cols, members)).astype(jnp.bfloat16)
+        copy_out(index).start()
+        return carry
+
+    lax.fori_loop(0, rows // chunk, update_chunk, 0)
+    for index in range(rows // chunk):
+        copy_out(index).wait()
+
+
+def analyse(priors, field, where, value, variance, noise, lon_count, lat_count):
+    rows, cols, members = field.shape
+    nobs = where.shape[2]
+    vmem, anywhere = pl.BlockSpec(memory_space=pltpu.VMEM), pl.BlockSpec(memory_space=pl.ANY)
+    return pl.pallas_call(
+        functools.partial(analysis_kernel, (lon_count, lat_count)),
+        out_shape=jax.ShapeDtypeStruct((rows, cols, members), jnp.bfloat16),
+        in_specs=[vmem, anywhere, vmem, vmem, vmem, vmem],
+        out_specs=anywhere,
+        scratch_shapes=[
+            pltpu.VMEM((rows, cols, members), jnp.float32),
+            pltpu.VMEM((2, rows * cols, BATCHES * nobs), jnp.bfloat16),
+            pltpu.VMEM((rows, cols, members), jnp.bfloat16),
+            pltpu.SemaphoreType.DMA,
+            pltpu.SemaphoreType.DMA((rows // 4,)),
+        ],
+        compiler_params=pltpu.CompilerParams(vmem_limit_bytes=32 * 1024 * 1024),
+        name="analyse",
+    )(priors, field, where, value, variance, noise)
 
 
 def body(ensemble_state, courant, obs_where, obs_value, obs_variance, obs_noise):
-    rows_tile, cols_tile, members = ensemble_state.shape
-    lat_count, lon_count = lax.axis_size("lat"), lax.axis_size("lon")
-    total_cols = cols_tile * lon_count
-    row_start = lax.axis_index("lat") * rows_tile
-    col_start = lax.axis_index("lon") * cols_tile
-    priors, field = gather(ensemble_state, courant, obs_where, lon_count, lat_count)
-    ensemble = field.reshape(rows_tile * cols_tile, members)
-    cell_index = jnp.arange(rows_tile * cols_tile, dtype=jnp.int32)
-    cell_lat = (row_start + cell_index // cols_tile)[:, None]
-    cell_lon = (col_start + cell_index % cols_tile)[:, None]
-
-    def update(cells, lat, lon, batch, anomaly_obs, weights):
-        taper = taper_weights(
-            lat, lon,
-            obs_where[batch, 0][None, :], obs_where[batch, 1][None, :], obs_where[batch, 2][None, :],
-            total_cols,
-        )
-        anomaly = cells - jnp.mean(cells, axis=1, keepdims=True)
-        covariance = matmul_exact(anomaly, anomaly_obs.T) / (members - 1)
-        return cells + matmul_exact(taper * covariance, weights)
-
-    for batch in range(BATCHES):
-        anomaly_obs, weights = batch_weights(
-            priors[batch], obs_value[batch], obs_variance[batch], obs_noise[batch]
-        )
-        ensemble = update(ensemble, cell_lat, cell_lon, batch, anomaly_obs, weights)
-        if batch + 1 < BATCHES:
-            later = update(
-                priors[batch + 1],
-                obs_where[batch + 1, 0][:, None], obs_where[batch + 1, 1][:, None],
-                batch, anomaly_obs, weights,
-            )
-            priors = priors.at[batch + 1].set(later)
-    return ensemble.reshape(rows_tile, cols_tile, members).astype(jnp.bfloat16)
+    counts = lax.axis_size("lon"), lax.axis_size("lat")
+    priors, field = gather(ensemble_state, courant, obs_where, *counts)
+    return analyse(priors, field, obs_where, obs_value, obs_variance, obs_noise, *counts)
 
 
 def solution(mesh):

time: 136 us -> 88.5 us (0.65)
  other arithmetic: 50.6 us -> 0 us
  Pallas kernels: 63.7 us -> 83.2 us
  matrix products: 15.5 us -> 0 us
    another operation x10 -> x0, other arithmetic: 46.7 us -> none  [the longest x6 25.8 us: batch_weights(): factor = jnp.linalg.cholesky(system)]
    pallas_call x0 -> x1, Pallas kernels: none -> 19.5 us  [analyse(): pl.pallas_call(functools.partial(analysis_kernel, (lon_count, lat_count))...]
    dot_general x8 -> x0, matrix products: 13.3 us -> none  [matmul_exact(): jnp.dot(left, right, precision=HIGHEST, preferred_element_type=jnp.float32)]
    sub x2 -> x0, other arithmetic: 2.25 us -> none  [the longest x1 1.68 us: update(): anomaly = cells - jnp.mean(cells, axis=1, keepdims=True)]
    unnamed x39 -> x11, local copies, waits for them, and re-layouts: 2.74 us -> 4.97 us
    another operation x4 -> x0, matrix products: 2.15 us -> none  [the longest x2 1.63 us: batch_weights(): lax.linalg.triangular_solve(factor, misfit, left_side=True, lower=True)]
where the time goes in v2:
time: 88.5 us; the launch traced here: 88.2 us
  Pallas kernels  83.2 us (94%)
  local copies, waits for them, and re-layouts  4.97 us (6%)
    pallas_call x1, Pallas kernels, gather(): pl.pallas_call(functools.partial(gather_kernel, (lon_count, lat_count)),...  63.7 us
    pallas_call x1, Pallas kernels, analyse(): pl.pallas_call(functools.partial(analysis_kernel, (lon_count, lat_count))...  19.5 us
    unnamed x11, local copies, waits for them, and re-layouts  4.97 us

profile of v2, /device:TPU:1, one launch (start us, length us, event | category | flops | bytes accessed | tf_op | source)
XLA Modules:
  0.0 88.2 jit_solution(14166837479699679396)
XLA Ops:
  0.0 0.7 copy.7.where_ref
  0.7 0.0 copy-start
  0.7 1.2 %copy-done = bf16[32,64,256]{2,1,0:T(8,128)(2,1)S(1)} copy-done((bf16[32,64,256]{2,1,0:T(8,128)(2,1)S(1)}, bf16[32,64,256]{2,1,0:T(8,128)(2,1)}, u32[]{:S(2)}) %copy-start) | copy-done | bytes 1048600
  1.9 0.0 copy-start.2
  1.9 0.8 copy-done.2
  2.7 63.7 %advance_and_gather.1 = (f32[2,128,256]{2,1,0:T(8,128)S(1)}, f32[32,64,256]{2,1,0:T(8,128)S(1)}) custom-call(bf16[32,64,256]{2,1,0:T(8,128)(2,1)S(1)} %copy-done, f32[2,32,64]{2,1,0:T(8,128)S(1)} %copy-done.2, s32[2,3,128]{2,1,0:T(4,128)S(1)} %copy.7.where_ref), custom_call_target="tpu_custom_call" | custom-call | tf_op jit(solution)/shard_map/advance_and_gather/pallas_call | solution.py:343
  66.4 0.0 copy-start.1
  66.4 0.9 %copy-done.1 = f32[2,128,256]{2,1,0:T(8,128)S(1)} copy-done((f32[2,128,256]{2,1,0:T(8,128)S(1)}, f32[2,128,256]{2,1,0:T(8,128)}, u32[]{:S(2)}) %copy-start.1) | copy-done | bytes 262168
  67.3 0.0 copy-start.3
  67.3 0.7 copy-done.3
  68.0 0.0 copy-start.4
  68.0 0.7 copy-done.4
  68.7 19.5 %analyse.1 = bf16[32,64,256]{2,1,0:T(8,128)(2,1)} custom-call(f32[2,128,256]{2,1,0:T(8,128)S(1)} %get-tuple-element.7.priors_ref, f32[32,64,256]{2,1,0:T(8,128)S(1)} %get-tuple-element.8.field_ref, s32[2,3,128]{2,1,0:T(4,128)S(1)} %copy.7.where_ref, f32[2,128]{1,0:T(2,128)S(1)} %copy-done.3, f32[2,128]{1,0:T(2,128)S(1)} %copy-done.4, ...), custom_call_target="tpu_custom_call" | custom-call | tf_op jit(solution)/shard_map/analyse/pallas_call | solution.py:579
Async XLA Ops:
  0.7 1.2 %copy-start = (bf16[32,64,256]{2,1,0:T(8,128)(2,1)S(1)}, bf16[32,64,256]{2,1,0:T(8,128)(2,1)}, u32[]{:S(2)}) copy-start(bf16[32,64,256]{2,1,0:T(8,128)(2,1)} %state_ref.1) | copy-start | bytes 3145732
  1.9 0.8 copy-start.2
  66.4 1.0 %copy-start.1 = (f32[2,128,256]{2,1,0:T(8,128)S(1)}, f32[2,128,256]{2,1,0:T(8,128)}, u32[]{:S(2)}) copy-start(f32[2,128,256]{2,1,0:T(8,128)} %noise_ref.1) | copy-start | bytes 786436
  67.3 0.7 copy-start.3
  68.0 0.7 copy-start.4

commit v3 on v2

--- a/solution.py
+++ b/solution.py
@@ -45,12 +45,25 @@
     }
 
 
+def ring_flips(count):
+    flips = [lambda place: place]
+    size = 1
+    while size < count:
+        flips += [lambda place, size=size, f=f: flip_bit(f(place), size) for f in flips]
+        size *= 2
+    return flips
+
+
+def flip_bit(place, size):
+    return place + size - 2 * size * (place // size % 2)
+
+
 def gather_kernel(
-    sizes, state_ref, courant_ref, where_ref,
+    sizes, state_hbm, courant_hbm, where_ref,
     priors_ref, field_ref,
-    near_ns, near_ew, near_corner, reach, wide, stencil, links, weights, part, pieces, piece, line, got,
-    grid, edge_send, edge_got,
-    near_sem, reach_sem, part_sem, line_sem, all_sem, send_sem, out_sem,
+    state_ref, courant_ref, near_ns, near_ew, near_corner, reach, wide, stencil, weights, part, pieces, piece, line, priors,
+    cells, bands, far_ns, far_ew, far_corner, field,
+    in_sem, near_sem, far_sem, part_sem, line_sem, all_sem, send_sem, out_sem,
 ):
     lon_count, lat_count = sizes
     plane_lon, line_lon, line_lat, plane_lat = split_mesh(lon_count, lat_count)
@@ -58,20 +71,43 @@
     rows, cols, members = state_ref.shape
     total_rows, total_cols = rows * lat_count, cols * lon_count
     nobs = where_ref.shape[2]
+    halves = members // LANES
+    band = nobs * halves // plane
     lon, lat = lax.axis_index("lon"), lax.axis_index("lat")
-    plane_me = (lon // line_lon) * plane_lat + lat % plane_lat
     line_me = (lat // plane_lat) * line_lon + lon % line_lon
-
-    def plane_device(index):
+    loads = [
+        pltpu.make_async_copy(courant_hbm, courant_ref, in_sem.at[0]),
+        pltpu.make_async_copy(state_hbm, state_ref, in_sem.at[1]),
+    ]
+    for load in loads:
+        load.start()
+
+    lon_flips, lat_flips = ring_flips(plane_lon), ring_flips(plane_lat)
+    plane_x = [flip(lon // line_lon) for flip in lon_flips]
+    plane_y = [flip(lat % plane_lat) for flip in lat_flips]
+    partners = [(i, j) for i in range(plane_lon) for j in range(plane_lat)][1:]
+    hops = {0: 0, 1: 1, 2: 2, 3: 1}
+    partners.sort(key=lambda p: -hops[p[0] % 4] - hops[p[1] // 2 % 4])
+    distances = sorted(range(1, lines), key=lambda d: -min(d, lines - d))
+
+    def plane_device(partner):
         return {
-            "lon": (index // plane_lat) * line_lon + lon % line_lon,
-            "lat": (lat // plane_lat) * plane_lat + index % plane_lat,
+            "lon": plane_x[partner[0]] * line_lon + lon % line_lon,
+            "lat": lat // plane_lat * plane_lat + plane_y[partner[1]],
         }
 
-    def line_device(index):
+    def tile_of(partner):
+        index = plane_x[partner[0]] * plane_lat + plane_y[partner[1]]
+        return (
+            pl.ds(pl.multiple_of(index // halves * band, band), band),
+            pl.ds(pl.multiple_of(index % halves * LANES, LANES), LANES),
+        )
+
+    def line_device(distance):
+        index = lax.rem(line_me + distance, lines)
         return {
-            "lon": (lon // line_lon) * line_lon + index % line_lon,
-            "lat": (index // line_lon) * plane_lat + lat % plane_lat,
+            "lon": lon // line_lon * line_lon + index % line_lon,
+            "lat": index // line_lon * plane_lat + lat % plane_lat,
         }
 
     def neighbour(lat_step, lon_step):
@@ -80,33 +116,29 @@
             "lat": lax.rem(lat + lat_step + lat_count, lat_count),
         }
 
-    around = [(a, b) for a in (-1, 0, 1) for b in (-1, 0, 1) if a or b]
+    around = [(a, b) for a in (-1, 1) for b in (0, -1, 1)] + [(0, -1), (0, 1)]
 
     barrier = pltpu.get_barrier_semaphore()
-    for step in around:
-        pl.semaphore_signal(barrier, inc=1, device_id=neighbour(*step), device_id_type=MESH)
-
-    def greet_line(d, carry):
-        target = line_device(lax.rem(line_me + d, lines))
+    greeted = [neighbour(*step) for step in around]
+    greeted += [line_device(distance) for distance in distances]
+    greeted += [plane_device(partner) for partner in partners]
+    for target in greeted:
         pl.semaphore_signal(barrier, inc=1, device_id=target, device_id_type=MESH)
-        return carry
-
-    def greet_plane(d, carry):
-        target = plane_device(lax.rem(plane_me + d, plane))
-        pl.semaphore_signal(barrier, inc=1, device_id=target, device_id_type=MESH)
-        return carry
-
-    lax.fori_loop(1, lines, greet_line, 0)
-    lax.fori_loop(1, plane, greet_plane, 0)
-
-    for r in range(rows):
-        grid[r + 2, PAD : PAD + cols, :] = state_ref[r].astype(jnp.float32)
-    for side, first in ((0, 0), (1, cols - 2)):
-        for j in range(2):
-            edge_send[side, j] = state_ref[:, first + j, :].astype(jnp.float32)
-    pl.semaphore_wait(barrier, len(around) + plane - 1 + lines - 1)
-
-    copies = []
+
+    for load in loads:
+        load.wait()
+    edges, ends = ((0, 2), (rows - 2, rows)), ((0, 2), (cols - 2, cols))
+    for side in range(2):
+        low, high = edges[side]
+        far_ns[side] = state_ref[low:high].astype(jnp.float32)
+        low, high = ends[side]
+        far_ew[side] = state_ref[:, low:high].astype(jnp.float32)
+        for other in range(2):
+            row, first = (0, rows - 1)[side], (0, cols - 8)[other]
+            far_corner[2 * side + other] = state_ref[row, first : first + 8].astype(jnp.float32)
+    cells[...] = jnp.zeros(cells.shape, jnp.bfloat16)
+    cells[2 : 2 + rows, :cols] = state_ref[...]
+    pl.semaphore_wait(barrier, len(greeted))
 
     def send(src, dst, sem, step):
         copy = pltpu.make_async_remote_copy(
@@ -114,7 +146,6 @@
             device_id=neighbour(*step), device_id_type=MESH,
         )
         copy.start()
-        copies.append(copy)
         return copy
 
     low, high = pl.ds(0, 8), pl.ds(rows - 8, 8)
@@ -130,19 +161,15 @@
         near.append(send(source, target, near_sem.at[index], (a, b)))
 
     far = []
-    inner = pl.ds(PAD, cols)
-    blocks = {
-        (1, 0): (grid.at[pl.ds(rows, 2), inner], grid.at[pl.ds(0, 2), inner]),
-        (-1, 0): (grid.at[pl.ds(2, 2), inner], grid.at[pl.ds(rows + 2, 2), inner]),
-        (0, 1): (edge_send.at[1], edge_got.at[0]),
-        (0, -1): (edge_send.at[0], edge_got.at[1]),
-        (1, 1): (grid.at[rows + 1, pl.ds(cols, 8)], grid.at[1, pl.ds(0, 8)]),
-        (1, -1): (grid.at[rows + 1, pl.ds(PAD, 8)], grid.at[1, pl.ds(PAD + cols, 8)]),
-        (-1, 1): (grid.at[2, pl.ds(cols, 8)], grid.at[rows + 2, pl.ds(0, 8)]),
-        (-1, -1): (grid.at[2, pl.ds(PAD, 8)], grid.at[rows + 2, pl.ds(PAD + cols, 8)]),
-    }
-    for index, step in enumerate(around):
-        far.append(send(*blocks[step], reach_sem.at[index], step))
+    for index, (a, b) in enumerate(around):
+        up, right = int(a > 0), int(b > 0)
+        if a and b:
+            source, target = far_corner.at[2 * up + right], far_corner.at[4 + 2 * (1 - up) + (1 - right)]
+        elif a:
+            source, target = far_ns.at[up], far_ns.at[2 + 1 - up]
+        else:
+            source, target = far_ew.at[right], far_ew.at[2 + 1 - right]
+        far.append(send(source, target, far_sem.at[index], (a, b)))
     for copy in near:
         copy.wait_recv()
 
@@ -152,14 +179,16 @@
         blank = jnp.zeros((8, LANES - cols), jnp.float32)
         own = jnp.concatenate([own, blank], axis=1)
         west = jnp.concatenate([blank, west], axis=1)
-        east = jnp.concatenate([blank, east], axis=1) if cols * 2 == LANES else None
+        east = jnp.concatenate([blank, east], axis=1)
         return jnp.where(lane < cols, own, jnp.where(lane < cols + 2, east, west))
 
     for c in range(2):
         reach[c, 0:8] = assemble(near_ns[0, c], near_corner[0, c], near_corner[1, c])
         for r in range(0, rows, 8):
-            band = pl.ds(r, 8)
-            reach[c, r + 8 : r + 16] = assemble(courant_ref[c, band], near_ew[0, c, band], near_ew[1, c, band])
+            band_rows = pl.ds(r, 8)
+            reach[c, r + 8 : r + 16] = assemble(
+                courant_ref[c, band_rows], near_ew[0, c, band_rows], near_ew[1, c, band_rows]
+            )
         reach[c, rows + 8 : rows + 16] = assemble(near_ns[1, c], near_corner[2, c], near_corner[3, c])
 
     row = lax.broadcasted_iota(jnp.int32, (rows + 16, LANES), 0) - 8 + lat * rows
@@ -174,18 +203,24 @@
             sums[total] = sums[total] + term if total in sums else term
     half = lax.broadcasted_iota(jnp.int32, (rows // 2, LANES), 1) < cols
     for index, total in enumerate(TWO_STEPS):
-        wide[index] = sums[total][8 : 8 + rows]
-        even = wide[index, pl.ds(0, rows // 2, 2), :]
-        odd = wide[index, pl.ds(1, rows // 2, 2), :]
+        wide[index] = sums[total]
+        even = wide[index, pl.ds(8, rows // 2, 2), :]
+        odd = wide[index, pl.ds(9, rows // 2, 2), :]
         stencil[index] = jnp.where(half, even, pltpu.roll(odd, cols, 1))
 
-    cells = rows * cols
+    def halves_into(ref, at, columns, value):
+        upper = value.astype(jnp.bfloat16)
+        count = value.shape[0]
+        ref[at : at + count, columns] = upper
+        ref[at + count : at + 2 * count, columns] = (value - upper.astype(jnp.float32)).astype(jnp.bfloat16)
+
     flat_lane = lax.broadcasted_iota(jnp.int32, (nobs, LANES), 1)
     second_row = jnp.where(flat_lane >= cols, 1, 0)
     column = flat_lane - second_row * cols
-    flat_state = state_ref[...].reshape(cells, members)
+    flat_state = state_ref[...].reshape(rows * cols, members)
     for batch in range(BATCHES):
-        where = jnp.concatenate([where_ref[batch], jnp.zeros((8 - 3, nobs), jnp.int32)], axis=0)
+        where = jnp.concatenate([where_ref[i, batch : batch + 1] for i in range(3)], axis=0)
+        where = jnp.concatenate([where, jnp.zeros((8 - 3, nobs), jnp.int32)], axis=0)
         where = jnp.transpose(where.astype(jnp.float32)).astype(jnp.int32)
         obs_row = where[:, 0:1] - lat * rows
         obs_col = where[:, 1:2] - lon * cols + 2
@@ -197,136 +232,90 @@
         def one_pair(pair, carry):
             lat_step = lat_base + 2 * pair
             total = jnp.zeros((nobs, LANES), jnp.float32)
-            for a in range(-2, 3):
-                for b in range(-2, 3):
-                    if (a, b) in TWO_STEPS:
-                        value = stencil[TWO_STEPS.index((a, b)), pl.ds(pair, 1), :]
-                        total = jnp.where((lat_step == a) & (lon_step == b), value, total)
-            upper = total.astype(jnp.bfloat16)
-            columns = pl.ds(pl.multiple_of(pair * LANES, LANES), LANES)
-            weights[0:nobs, columns] = upper
-            weights[nobs : 2 * nobs, columns] = (total - upper.astype(jnp.float32)).astype(jnp.bfloat16)
+            for index, (a, b) in enumerate(TWO_STEPS):
+                total = jnp.where((lat_step == a) & (lon_step == b), stencil[index, pl.ds(pair, 1), :], total)
+            halves_into(weights, 0, pl.ds(pl.multiple_of(pair * LANES, LANES), LANES), total)
             return carry
 
         lax.fori_loop(0, rows // 2, one_pair, 0)
         share = jnp.dot(weights[...], flat_state, preferred_element_type=jnp.float32)
         part[batch] = share[:nobs] + share[nobs:]
-
-        def send_part(d, carry):
-            index = lax.rem(plane_me + d, plane)
-            copy = pltpu.make_async_remote_copy(
-                src_ref=part.at[batch, *tile_of(index)], dst_ref=pieces.at[batch, d],
+        for index, partner in enumerate(partners):
+            pltpu.make_async_remote_copy(
+                src_ref=part.at[batch, *tile_of(partner)], dst_ref=pieces.at[batch, index],
                 send_sem=send_sem.at[batch, 0], recv_sem=part_sem.at[batch],
-                device_id=plane_device(index), device_id_type=MESH,
-            )
-            copy.start()
-            return carry
-
-        def tile_of(index):
-            halves = members // LANES
-            band = nobs * halves // plane
-            return (
-                pl.ds(pl.multiple_of((index // halves) * band, band), band),
-                pl.ds(pl.multiple_of((index % halves) * LANES, LANES), LANES),
-            )
-
-        lax.fori_loop(1, plane, send_part, 0)
-
+                device_id=plane_device(partner), device_id_type=MESH,
+            ).start()
+
+    mine = tile_of((0, 0))
     for batch in range(BATCHES):
-        pltpu.make_async_copy(pieces.at[batch, 1:plane], pieces.at[batch, 1:plane], part_sem.at[batch]).wait()
-        piece[batch] = part[batch, *tile_of(plane_me)] + jnp.sum(pieces[batch, 1:plane], axis=0)
-
-        def send_line(d, carry):
-            copy = pltpu.make_async_remote_copy(
-                src_ref=piece.at[batch], dst_ref=line.at[batch, d],
+        pltpu.make_async_copy(pieces.at[batch], pieces.at[batch], part_sem.at[batch]).wait()
+        piece[batch] = part[batch, *mine] + jnp.sum(pieces[batch], axis=0)
+        for index, distance in enumerate(distances):
+            pltpu.make_async_remote_copy(
+                src_ref=piece.at[batch], dst_ref=line.at[batch, index],
                 send_sem=send_sem.at[batch, 1], recv_sem=line_sem.at[batch],
-                device_id=line_device(lax.rem(line_me + d, lines)), device_id_type=MESH,
-            )
-            copy.start()
-            return carry
-
-        lax.fori_loop(1, lines, send_line, 0)
+                device_id=line_device(distance), device_id_type=MESH,
+            ).start()
 
     for copy in far:
         copy.wait_recv()
-    for side, first in ((0, PAD - 2), (1, PAD + cols)):
-        for j in range(2):
-            grid[2 : 2 + rows, first + j, :] = edge_got[side, j]
-    width = cols + 2 * PAD
-    for index, step in enumerate(ONE_STEP):
-        upright = jnp.concatenate([weight[step], jnp.zeros((LANES - rows - 16, LANES), jnp.float32)], axis=0)
-        links[index] = jnp.transpose(pltpu.roll(upright, PAD, 1))[:width]
-
-    def one_row(r, source, target):
-        rolled = [
-            jnp.broadcast_to(pltpu.roll(links[i], lax.rem(LANES - r - 6, LANES), 1)[:, 0:1], (width, LANES))
-            for i in range(len(ONE_STEP))
-        ]
-        for first in range(0, members, LANES):
-            lanes = pl.ds(first, LANES)
-            here = source[r, :, lanes]
-            target(
-                r, lanes,
-                rolled[0] * here
-                + rolled[1] * source[r - 1, :, lanes]
-                + rolled[2] * source[r + 1, :, lanes]
-                + rolled[3] * pltpu.roll(here, 1, 0)
-                + rolled[4] * pltpu.roll(here, width - 1, 0),
-            )
-
-    def first_row(r, carry):
-        def store(r, lanes, value):
-            halfway[r, :, lanes] = value
-
-        one_row(r, grid, store)
+    gap = jnp.zeros((14, members), jnp.float32)
+
+    def beside(at, west, east):
+        cells[at, cols : cols + 16] = jnp.concatenate([east, gap], axis=0).astype(jnp.bfloat16)
+        cells[at, LANES - 16 :] = jnp.concatenate([gap, west], axis=0).astype(jnp.bfloat16)
+
+    def beside_row(r, carry):
+        beside(r + 2, far_ew[2, r], far_ew[3, r])
         return carry
 
-    halfway = got[1]
-    lax.fori_loop(1, rows + 3, first_row, 0)
-
-    def second_row_of(r, carry):
-        def store(r, lanes, value):
-            grid[r, :, lanes] = value
-
-        one_row(r, halfway, store)
+    lax.fori_loop(0, rows, beside_row, 0)
+    for side, at in ((0, 1), (1, rows + 2)):
+        cells[(0, rows + 2)[side] : (2, rows + 4)[side], :cols] = far_ns[2 + side].astype(jnp.bfloat16)
+        beside(at, far_corner[4 + 2 * side, 6:8], far_corner[4 + 2 * side + 1, 0:2])
+    step_lane = lax.broadcasted_iota(jnp.int32, (cols, LANES), 1) - lax.broadcasted_iota(jnp.int32, (cols, LANES), 0)
+    step_lane = jnp.where(step_lane > LANES // 2 + 2, step_lane - LANES, step_lane)
+
+    def one_pair_of_rows(pair, carry):
+        first = 2 * pair
+        for around_row in range(6):
+            for r in range(2):
+                a = around_row - 2 - r
+                total = jnp.zeros((cols, LANES), jnp.float32)
+                if -2 <= a <= 2:
+                    for index, (lat_step, b) in enumerate(TWO_STEPS):
+                        if lat_step == a:
+                            total = jnp.where(step_lane == b, wide[index, pl.ds(first + around_row + 6, 1), :], total)
+                halves_into(bands, 2 * r * cols, pl.ds(around_row * LANES, LANES), total)
+        near_cells = cells[pl.ds(first, 6)].reshape(6 * LANES, members)
+        result = jnp.dot(bands[...], near_cells, preferred_element_type=jnp.float32)
+        for r in range(2):
+            field[first + r] = result[2 * r * cols : (2 * r + 1) * cols] + result[(2 * r + 1) * cols : (2 * r + 2) * cols]
         return carry
 
-    for copy in far:
-        copy.wait_send()
-    lax.fori_loop(2, rows + 2, second_row_of, 0)
-    out = pltpu.make_async_copy(grid.at[pl.ds(2, rows), pl.ds(PAD, cols)], field_ref, out_sem)
+    lax.fori_loop(0, rows // 2, one_pair_of_rows, 0)
+    out = pltpu.make_async_copy(field, field_ref, out_sem)
     out.start()
 
-    priors = got[0]
     for batch in range(BATCHES):
-        pltpu.make_async_copy(line.at[batch, 1:lines], line.at[batch, 1:lines], line_sem.at[batch]).wait()
-        mine = tile_of(plane_me)
-        priors[batch, *mine] = piece[batch] + jnp.sum(line[batch, 1:lines], axis=0)
-
-        def send_all(d, carry):
-            copy = pltpu.make_async_remote_copy(
+        pltpu.make_async_copy(line.at[batch], line.at[batch], line_sem.at[batch]).wait()
+        priors[batch, *mine] = piece[batch] + jnp.sum(line[batch], axis=0)
+        for partner in partners:
+            pltpu.make_async_remote_copy(
                 src_ref=priors.at[batch, *mine], dst_ref=priors.at[batch, *mine],
                 send_sem=send_sem.at[batch, 2], recv_sem=all_sem.at[batch],
-                device_id=plane_device(lax.rem(plane_me + d, plane)), device_id_type=MESH,
-            )
-            copy.start()
-            return carry
-
-        lax.fori_loop(1, plane, send_all, 0)
+                device_id=plane_device(partner), device_id_type=MESH,
+            ).start()
     for batch in range(BATCHES):
-        block = pieces.at[batch, 1:plane]
-        pltpu.make_async_copy(block, block, all_sem.at[batch]).wait()
+        pltpu.make_async_copy(pieces.at[batch], pieces.at[batch], all_sem.at[batch]).wait()
         priors_ref[batch] = priors[batch]
 
-    for copy in near:
+    for copy in near + far:
         copy.wait_send()
     for batch in range(BATCHES):
-        block = pieces.at[batch, 1:plane]
-        pltpu.make_async_copy(block, block, send_sem.at[batch, 0]).wait()
-        block = line.at[batch, 1:lines]
-        pltpu.make_async_copy(block, block, send_sem.at[batch, 1]).wait()
-        block = pieces.at[batch, 1:plane]
-        pltpu.make_async_copy(block, block, send_sem.at[batch, 2]).wait()
+        for sem, sent in enumerate((pieces, line, pieces)):
+            pltpu.make_async_copy(sent.at[batch], sent.at[batch], send_sem.at[batch, sem]).wait()
     out.wait()
 
 
@@ -336,9 +325,8 @@
     plane_lon, line_lon, line_lat, plane_lat = split_mesh(lon_count, lat_count)
     plane, lines = plane_lon * plane_lat, line_lat * line_lon
     band = nobs * (members // LANES) // plane
-    width = cols + 2 * PAD
-    f32 = jnp.float32
-    vmem = pl.BlockSpec(memory_space=pltpu.VMEM)
+    f32, bf16 = jnp.float32, jnp.bfloat16
+    vmem, hbm = pl.BlockSpec(memory_space=pltpu.VMEM), pl.BlockSpec(memory_space=pltpu.HBM)
     dma = pltpu.SemaphoreType.DMA
     return pl.pallas_call(
         functools.partial(gather_kernel, (lon_count, lat_count)),
@@ -346,25 +334,30 @@
             jax.ShapeDtypeStruct((BATCHES, nobs, members), f32),
             jax.ShapeDtypeStruct((rows, cols, members), f32),
         ),
-        in_specs=[vmem] * 3,
+        in_specs=[hbm, hbm, vmem],
         out_specs=(vmem, pl.BlockSpec(memory_space=pl.ANY)),
         scratch_shapes=[
+            pltpu.VMEM((rows, cols, members), bf16),
+            pltpu.VMEM((2, rows, cols), f32),
             pltpu.VMEM((2, 2, 8, cols), f32),
             pltpu.VMEM((2, 2, rows, cols), f32),
             pltpu.VMEM((4, 2, 8, cols), f32),
             pltpu.VMEM((2, rows + 16, LANES), f32),
-            pltpu.VMEM((len(TWO_STEPS), rows, LANES), f32),
+            pltpu.VMEM((len(TWO_STEPS), rows + 16, LANES), f32),
             pltpu.VMEM((len(TWO_STEPS), rows // 2, LANES), f32),
-            pltpu.VMEM((len(ONE_STEP), width, LANES), f32),
-            pltpu.VMEM((2 * nobs, rows * cols), jnp.bfloat16),
+            pltpu.VMEM((2 * nobs, rows * cols), bf16),
             pltpu.VMEM((BATCHES, nobs, members), f32),
-            pltpu.VMEM((BATCHES, plane, band, LANES), f32),
+            pltpu.VMEM((BATCHES, plane - 1, band, LANES), f32),
             pltpu.VMEM((BATCHES, band, LANES), f32),
-            pltpu.VMEM((BATCHES, lines, band, LANES), f32),
-            [pltpu.VMEM((BATCHES, nobs, members), f32), pltpu.VMEM((rows + 4, width, members), f32)],
-            pltpu.VMEM((rows + 4, width, members), f32),
-            pltpu.VMEM((2, 2, rows, members), f32),
-            pltpu.VMEM((2, 2, rows, members), f32),
+            pltpu.VMEM((BATCHES, lines - 1, band, LANES), f32),
+            pltpu.VMEM((BATCHES, nobs, members), f32),
+            pltpu.VMEM((rows + 4, LANES, members), bf16),
+            pltpu.VMEM((4 * cols, 6 * LANES), bf16),
+            pltpu.VMEM((4, 2, cols, members), f32),
+            pltpu.VMEM((4, rows, 2, members), f32),
+            pltpu.VMEM((8, 8, members), f32),
+            pltpu.VMEM((rows, cols, members), f32),
+            dma((2,)),
             dma((8, 2)),
             dma((8, 2)),
             dma((BATCHES,)),
@@ -374,7 +367,7 @@
             dma,
         ],
         compiler_params=pltpu.CompilerParams(
-            collective_id=0, has_side_effects=True, vmem_limit_bytes=48 * 1024 * 1024
+            collective_id=0, has_side_effects=True, vmem_limit_bytes=40 * 1024 * 1024
         ),
         name="advance_and_gather",
     )(state, courant, where)
@@ -509,13 +502,13 @@
     def centred(priors):
         return priors - jnp.mean(priors, axis=1, keepdims=True)
 
-    obs = [[where_ref[batch, i : i + 1, :] for i in range(3)] for batch in range(BATCHES)]
+    obs = [[where_ref[i, batch : batch + 1, :] for i in range(3)] for batch in range(BATCHES)]
     priors = [priors_ref[batch] for batch in range(BATCHES)]
     anomaly, weights = [centred(priors[0])], []
     weights.append(weights_of(0, priors[0], anomaly[0]))
 
-    where = jnp.concatenate([where_ref[1].astype(jnp.float32), jnp.zeros((8 - 3, nobs), jnp.float32)], axis=0)
-    where = jnp.transpose(where).astype(jnp.int32)
+    where = jnp.concatenate(obs[1] + [jnp.zeros((8 - 3, nobs), jnp.int32)], axis=0)
+    where = jnp.transpose(where.astype(jnp.float32)).astype(jnp.int32)
     lat_gap = where[:, 0:1] - obs[0][0]
     lon_gap = lon_distance(where[:, 1:2], obs[0][1])
     distance = (square(lat_gap) + square(lon_gap)).astype(jnp.float32)
@@ -595,8 +588,9 @@
 
 def body(ensemble_state, courant, obs_where, obs_value, obs_variance, obs_noise):
     counts = lax.axis_size("lon"), lax.axis_size("lat")
-    priors, field = gather(ensemble_state, courant, obs_where, *counts)
-    return analyse(priors, field, obs_where, obs_value, obs_variance, obs_noise, *counts)
+    where = jnp.transpose(obs_where, (1, 0, 2))
+    priors, field = gather(ensemble_state, courant, where, *counts)
+    return analyse(priors, field, where, obs_value, obs_variance, obs_noise, *counts)
 
 
 def solution(mesh):

time: 88.5 us -> 77.3 us (0.87)
  Pallas kernels: 83.2 us -> 72 us
    pallas_call x1, Pallas kernels: 63.7 us -> 52.5 us  [gather(): pl.pallas_call(functools.partial(gather_kernel, (lon_count, lat_count)),...]
    unnamed x11 -> x12, local copies, waits for them, and re-layouts: 4.97 us -> 4.97 us
where the time goes in v3:
time: 77.3 us; the launch traced here: 77 us
  Pallas kernels  72 us (93%)
  local copies, waits for them, and re-layouts  4.97 us (6%)
    pallas_call x1, Pallas kernels, gather(): pl.pallas_call(functools.partial(gather_kernel, (lon_count, lat_count)),...  52.5 us
    pallas_call x1, Pallas kernels, analyse(): pl.pallas_call(functools.partial(analysis_kernel, (lon_count, lat_count))...  19.5 us
    unnamed x12, local copies, waits for them, and re-layouts  4.97 us

profile of v3, /device:TPU:1, one launch (start us, length us, event | category | flops | bytes accessed | tf_op | source)
XLA Modules:
  0.0 77.0 jit_solution(6811077869247376007)
XLA Ops:
  0.0 0.0 copy-start
  0.0 1.2 %copy-done = bf16[32,64,256]{2,1,0:T(8,128)(2,1)S(1)} copy-done((bf16[32,64,256]{2,1,0:T(8,128)(2,1)S(1)}, bf16[32,64,256]{2,1,0:T(8,128)(2,1)}, u32[]{:S(2)}) %copy-start) | copy-done | bytes 1048600
  1.2 0.0 copy-start.2
  1.2 0.8 copy-done.2
  2.0 0.0 copy-start.3
  2.0 0.7 copy-done.3
  2.7 52.5 %advance_and_gather.1 = (f32[2,128,256]{2,1,0:T(8,128)S(1)}, f32[32,64,256]{2,1,0:T(8,128)S(1)}) custom-call(bf16[32,64,256]{2,1,0:T(8,128)(2,1)S(1)} %copy-done, f32[2,32,64]{2,1,0:T(8,128)S(1)} %copy-done.2, s32[3,2,128]{2,1,0:T(2,128)S(1)} %bitcast.1), custom_call_target="tpu_custom_call" | custom-call | tf_op jit(solution)/shard_map/advance_and_gather/pallas_call | solution.py:331
  55.2 0.0 copy-start.1
  55.2 0.9 %copy-done.1 = f32[2,128,256]{2,1,0:T(8,128)S(1)} copy-done((f32[2,128,256]{2,1,0:T(8,128)S(1)}, f32[2,128,256]{2,1,0:T(8,128)}, u32[]{:S(2)}) %copy-start.1) | copy-done | bytes 262168
  56.1 0.0 copy-start.4
  56.1 0.7 copy-done.4
  56.8 0.0 copy-start.5
  56.8 0.7 copy-done.5
  57.5 19.5 %analyse.1 = bf16[32,64,256]{2,1,0:T(8,128)(2,1)} custom-call(f32[2,128,256]{2,1,0:T(8,128)S(1)} %get-tuple-element.7.priors_ref, f32[32,64,256]{2,1,0:T(8,128)S(1)} %get-tuple-element.8.field_ref, s32[3,2,128]{2,1,0:T(2,128)S(1)} %bitcast.2, f32[2,128]{1,0:T(2,128)S(1)} %copy-done.4, f32[2,128]{1,0:T(2,128)S(1)} %copy-done.5, f32[2,128,256]{2,1,0:T(8,128)S(1)} %copy-done.1), custom_call_target="tpu_custom_call" | custom-call | tf_op jit(solution)/shard_map/analyse/pallas_call | solution.py:572
Async XLA Ops:
  0.0 1.2 %copy-start = (bf16[32,64,256]{2,1,0:T(8,128)(2,1)S(1)}, bf16[32,64,256]{2,1,0:T(8,128)(2,1)}, u32[]{:S(2)}) copy-start(bf16[32,64,256]{2,1,0:T(8,128)(2,1)} %state_hbm.1) | copy-start | bytes 3145732
  1.2 0.8 copy-start.2
  2.0 0.7 copy-start.3
  55.2 1.0 %copy-start.1 = (f32[2,128,256]{2,1,0:T(8,128)S(1)}, f32[2,128,256]{2,1,0:T(8,128)}, u32[]{:S(2)}) copy-start(f32[2,128,256]{2,1,0:T(8,128)} %noise_ref.1) | copy-start | bytes 786436
  56.1 0.7 copy-start.4
  56.8 0.7 copy-start.5

commit v4 on v3

--- a/solution.py
+++ b/solution.py
@@ -8,7 +8,7 @@
 
 BATCHES = 2
 MESH = pl.DeviceIdType.MESH
-PAD = 8
+VMEM_BYTES = 63 * 1024 * 1024
 LANES = 128
 HIGHEST = lax.Precision.HIGHEST
 ONE_STEP = ((0, 0), (-1, 0), (1, 0), (0, -1), (0, 1))
@@ -58,11 +58,11 @@
     return place + size - 2 * size * (place // size % 2)
 
 
-def gather_kernel(
-    sizes, state_hbm, courant_hbm, where_ref,
-    priors_ref, field_ref,
-    state_ref, courant_ref, near_ns, near_ew, near_corner, reach, wide, stencil, weights, part, pieces, piece, line, priors,
-    cells, bands, far_ns, far_ew, far_corner, field,
+def window_kernel(
+    sizes, state_hbm, courant_hbm, where_hbm, value_hbm, variance_hbm, noise_hbm, out_ref,
+    state_ref, courant_ref, where_ref, value_ref, variance_ref, noise_ref,
+    near_ns, near_ew, near_corner, reach, wide, stencil, weights, part, pieces, piece, line, priors,
+    cells, bands, far_ns, far_ew, far_corner, field, spread, analysis,
     in_sem, near_sem, far_sem, part_sem, line_sem, all_sem, send_sem, out_sem,
 ):
     lon_count, lat_count = sizes
@@ -75,10 +75,11 @@
     band = nobs * halves // plane
     lon, lat = lax.axis_index("lon"), lax.axis_index("lat")
     line_me = (lat // plane_lat) * line_lon + lon % line_lon
-    loads = [
-        pltpu.make_async_copy(courant_hbm, courant_ref, in_sem.at[0]),
-        pltpu.make_async_copy(state_hbm, state_ref, in_sem.at[1]),
-    ]
+    arguments = (
+        (courant_hbm, courant_ref), (state_hbm, state_ref), (where_hbm, where_ref),
+        (value_hbm, value_ref), (variance_hbm, variance_ref), (noise_hbm, noise_ref),
+    )
+    loads = [pltpu.make_async_copy(*pair, in_sem.at[index]) for index, pair in enumerate(arguments)]
     for load in loads:
         load.start()
 
@@ -295,8 +296,6 @@
         return carry
 
     lax.fori_loop(0, rows // 2, one_pair_of_rows, 0)
-    out = pltpu.make_async_copy(field, field_ref, out_sem)
-    out.start()
 
     for batch in range(BATCHES):
         pltpu.make_async_copy(line.at[batch], line.at[batch], line_sem.at[batch]).wait()
@@ -307,70 +306,19 @@
                 send_sem=send_sem.at[batch, 2], recv_sem=all_sem.at[batch],
                 device_id=plane_device(partner), device_id_type=MESH,
             ).start()
-    for batch in range(BATCHES):
+    def arrival(batch):
         pltpu.make_async_copy(pieces.at[batch], pieces.at[batch], all_sem.at[batch]).wait()
-        priors_ref[batch] = priors[batch]
+        return priors[batch]
+
+    analyse(
+        sizes, arrival, where_ref, value_ref, variance_ref, noise_ref, out_ref, field, spread, analysis, out_sem
+    )
 
     for copy in near + far:
         copy.wait_send()
     for batch in range(BATCHES):
         for sem, sent in enumerate((pieces, line, pieces)):
             pltpu.make_async_copy(sent.at[batch], sent.at[batch], send_sem.at[batch, sem]).wait()
-    out.wait()
-
-
-def gather(state, courant, where, lon_count, lat_count):
-    rows, cols, members = state.shape
-    nobs = where.shape[2]
-    plane_lon, line_lon, line_lat, plane_lat = split_mesh(lon_count, lat_count)
-    plane, lines = plane_lon * plane_lat, line_lat * line_lon
-    band = nobs * (members // LANES) // plane
-    f32, bf16 = jnp.float32, jnp.bfloat16
-    vmem, hbm = pl.BlockSpec(memory_space=pltpu.VMEM), pl.BlockSpec(memory_space=pltpu.HBM)
-    dma = pltpu.SemaphoreType.DMA
-    return pl.pallas_call(
-        functools.partial(gather_kernel, (lon_count, lat_count)),
-        out_shape=(
-            jax.ShapeDtypeStruct((BATCHES, nobs, members), f32),
-            jax.ShapeDtypeStruct((rows, cols, members), f32),
-        ),
-        in_specs=[hbm, hbm, vmem],
-        out_specs=(vmem, pl.BlockSpec(memory_space=pl.ANY)),
-        scratch_shapes=[
-            pltpu.VMEM((rows, cols, members), bf16),
-            pltpu.VMEM((2, rows, cols), f32),
-            pltpu.VMEM((2, 2, 8, cols), f32),
-            pltpu.VMEM((2, 2, rows, cols), f32),
-            pltpu.VMEM((4, 2, 8, cols), f32),
-            pltpu.VMEM((2, rows + 16, LANES), f32),
-            pltpu.VMEM((len(TWO_STEPS), rows + 16, LANES), f32),
-            pltpu.VMEM((len(TWO_STEPS), rows // 2, LANES), f32),
-            pltpu.VMEM((2 * nobs, rows * cols), bf16),
-            pltpu.VMEM((BATCHES, nobs, members), f32),
-            pltpu.VMEM((BATCHES, plane - 1, band, LANES), f32),
-            pltpu.VMEM((BATCHES, band, LANES), f32),
-            pltpu.VMEM((BATCHES, lines - 1, band, LANES), f32),
-            pltpu.VMEM((BATCHES, nobs, members), f32),
-            pltpu.VMEM((rows + 4, LANES, members), bf16),
-            pltpu.VMEM((4 * cols, 6 * LANES), bf16),
-            pltpu.VMEM((4, 2, cols, members), f32),
-            pltpu.VMEM((4, rows, 2, members), f32),
-            pltpu.VMEM((8, 8, members), f32),
-            pltpu.VMEM((rows, cols, members), f32),
-            dma((2,)),
-            dma((8, 2)),
-            dma((8, 2)),
-            dma((BATCHES,)),
-            dma((BATCHES,)),
-            dma((BATCHES,)),
-            dma((BATCHES, 3)),
-            dma,
-        ],
-        compiler_params=pltpu.CompilerParams(
-            collective_id=0, has_side_effects=True, vmem_limit_bytes=40 * 1024 * 1024
-        ),
-        name="advance_and_gather",
-    )(state, courant, where)
 
 
 def matmul_exact(left, right, contract=(1, 0)):
@@ -469,17 +417,14 @@
     return value * value
 
 
-def analysis_kernel(
-    sizes, priors_ref, field_ref, where_ref, value_ref, variance_ref, noise_ref, out_ref,
-    field, spread, analysis, field_sem, out_sem,
+def analyse(
+    sizes, arrival, where_ref, value_ref, variance_ref, noise_ref, out_ref, field, spread, analysis, out_sem
 ):
     lon_count, lat_count = sizes
-    rows, cols, members = field_ref.shape
+    rows, cols, members = field.shape
     nobs = where_ref.shape[2]
     total_cols = cols * lon_count
     first_row, first_col = lax.axis_index("lat") * rows, lax.axis_index("lon") * cols
-    fetch = pltpu.make_async_copy(field_ref, field, field_sem)
-    fetch.start()
 
     blank = jnp.zeros((8 - 2 * BATCHES, nobs), jnp.float32)
     upright = jnp.transpose(jnp.concatenate([value_ref[...], variance_ref[...], blank], axis=0))
@@ -503,7 +448,7 @@
         return priors - jnp.mean(priors, axis=1, keepdims=True)
 
     obs = [[where_ref[i, batch : batch + 1, :] for i in range(3)] for batch in range(BATCHES)]
-    priors = [priors_ref[batch] for batch in range(BATCHES)]
+    priors = [arrival(0)]
     anomaly, weights = [centred(priors[0])], []
     weights.append(weights_of(0, priors[0], anomaly[0]))
 
@@ -513,8 +458,9 @@
     lon_gap = lon_distance(where[:, 1:2], obs[0][1])
     distance = (square(lat_gap) + square(lon_gap)).astype(jnp.float32)
     taper = square(jnp.maximum(1.0 - distance / square(obs[0][2]).astype(jnp.float32), 0.0))
-    covariance = matmul_exact(centred(priors[1]), anomaly[0], (1, 1)) / (members - 1)
-    priors[1] += matmul_exact(taper * covariance, weights[0])
+    before = arrival(1)
+    covariance = matmul_exact(centred(before), anomaly[0], (1, 1)) / (members - 1)
+    priors.append(before + matmul_exact(taper * covariance, weights[0]))
     anomaly.append(centred(priors[1]))
     carried = halves_of(matmul_exact(centred(weights[0]), anomaly[1], (1, 1)) / (members - 1))
 
@@ -522,7 +468,6 @@
     cell_lon = first_col + lax.broadcasted_iota(jnp.int32, (cols, 1), 0)
     lon_part = [scaled_square(lon_distance(cell_lon, lon), radius) for _, lon, radius in obs]
     chunk = 4
-    fetch.wait()
 
     def taper_of(batch, row):
         lat, _, radius = obs[batch]
@@ -565,32 +510,63 @@
         copy_out(index).wait()
 
 
-def analyse(priors, field, where, value, variance, noise, lon_count, lat_count):
-    rows, cols, members = field.shape
+def window(state, courant, where, value, variance, noise, lon_count, lat_count):
+    rows, cols, members = state.shape
     nobs = where.shape[2]
-    vmem, anywhere = pl.BlockSpec(memory_space=pltpu.VMEM), pl.BlockSpec(memory_space=pl.ANY)
+    plane_lon, line_lon, line_lat, plane_lat = split_mesh(lon_count, lat_count)
+    plane, lines = plane_lon * plane_lat, line_lat * line_lon
+    band = nobs * (members // LANES) // plane
+    f32, bf16 = jnp.float32, jnp.bfloat16
+    anywhere = pl.BlockSpec(memory_space=pl.ANY)
+    dma = pltpu.SemaphoreType.DMA
+    arguments = (state, courant, where, value, variance, noise)
     return pl.pallas_call(
-        functools.partial(analysis_kernel, (lon_count, lat_count)),
-        out_shape=jax.ShapeDtypeStruct((rows, cols, members), jnp.bfloat16),
-        in_specs=[vmem, anywhere, vmem, vmem, vmem, vmem],
+        functools.partial(window_kernel, (lon_count, lat_count)),
+        out_shape=jax.ShapeDtypeStruct((rows, cols, members), bf16),
+        in_specs=[anywhere] * len(arguments),
         out_specs=anywhere,
-        scratch_shapes=[
-            pltpu.VMEM((rows, cols, members), jnp.float32),
-            pltpu.VMEM((2, rows * cols, BATCHES * nobs), jnp.bfloat16),
-            pltpu.VMEM((rows, cols, members), jnp.bfloat16),
-            pltpu.SemaphoreType.DMA,
-            pltpu.SemaphoreType.DMA((rows // 4,)),
+        scratch_shapes=[pltpu.VMEM(argument.shape, argument.dtype) for argument in arguments]
+        + [
+            pltpu.VMEM((2, 2, 8, cols), f32),
+            pltpu.VMEM((2, 2, rows, cols), f32),
+            pltpu.VMEM((4, 2, 8, cols), f32),
+            pltpu.VMEM((2, rows + 16, LANES), f32),
+            pltpu.VMEM((len(TWO_STEPS), rows + 16, LANES), f32),
+            pltpu.VMEM((len(TWO_STEPS), rows // 2, LANES), f32),
+            pltpu.VMEM((2 * nobs, rows * cols), bf16),
+            pltpu.VMEM((BATCHES, nobs, members), f32),
+            pltpu.VMEM((BATCHES, plane - 1, band, LANES), f32),
+            pltpu.VMEM((BATCHES, band, LANES), f32),
+            pltpu.VMEM((BATCHES, lines - 1, band, LANES), f32),
+            pltpu.VMEM((BATCHES, nobs, members), f32),
+            pltpu.VMEM((rows + 4, LANES, members), bf16),
+            pltpu.VMEM((4 * cols, 6 * LANES), bf16),
+            pltpu.VMEM((4, 2, cols, members), f32),
+            pltpu.VMEM((4, rows, 2, members), f32),
+            pltpu.VMEM((8, 8, members), f32),
+            pltpu.VMEM((rows, cols, members), f32),
+            pltpu.VMEM((2, rows * cols, BATCHES * nobs), bf16),
+            pltpu.VMEM((rows, cols, members), bf16),
+            dma((len(arguments),)),
+            dma((8, 2)),
+            dma((8, 2)),
+            dma((BATCHES,)),
+            dma((BATCHES,)),
+            dma((BATCHES,)),
+            dma((BATCHES, 3)),
+            dma((rows // 4,)),
         ],
-        compiler_params=pltpu.CompilerParams(vmem_limit_bytes=32 * 1024 * 1024),
-        name="analyse",
-    )(priors, field, where, value, variance, noise)
+        compiler_params=pltpu.CompilerParams(
+            collective_id=0, has_side_effects=True, vmem_limit_bytes=VMEM_BYTES
+        ),
+        name="window",
+    )(*arguments)
 
 
 def body(ensemble_state, courant, obs_where, obs_value, obs_variance, obs_noise):
     counts = lax.axis_size("lon"), lax.axis_size("lat")
     where = jnp.transpose(obs_where, (1, 0, 2))
-    priors, field = gather(ensemble_state, courant, where, *counts)
-    return analyse(priors, field, where, obs_value, obs_variance, obs_noise, *counts)
+    return window(ensemble_state, courant, where, obs_value, obs_variance, obs_noise, *counts)
 
 
 def solution(mesh):

time: 77.3 us -> 73.4 us (0.950)
  local copies, waits for them, and re-layouts: 4.97 us -> 2.3 us
  Pallas kernels: 72 us -> 70.9 us
    unnamed x12 -> x1, local copies, waits for them, and re-layouts: 4.97 us -> 2.3 us
    pallas_call x2 -> x1, Pallas kernels: 72 us -> 70.9 us  [window(): pl.pallas_call(functools.partial(window_kernel, (lon_count, lat_count)),...]
where the time goes in v4:
time: 73.4 us; the launch traced here: 73.2 us
  Pallas kernels  70.9 us (97%)
  local copies, waits for them, and re-layouts  2.3 us (3%)
    pallas_call x1, Pallas kernels, window(): pl.pallas_call(functools.partial(window_kernel, (lon_count, lat_count)),...  70.9 us
    unnamed x1, local copies, waits for them, and re-layouts  2.3 us

profile of v4, /device:TPU:1, one launch (start us, length us, event | category | flops | bytes accessed | tf_op | source)
XLA Modules:
  0.0 73.2 jit_solution(3344642407150449781)
XLA Ops:
  0.0 70.9 %window.1 = bf16[32,64,256]{2,1,0:T(8,128)(2,1)} custom-call(bf16[32,64,256]{2,1,0:T(8,128)(2,1)} %state_hbm.1, f32[2,32,64]{2,1,0:T(8,128)} %courant_hbm.1, s32[3,2,128]{2,1,0:T(2,128)} %bitcast.1, f32[2,128]{1,0:T(2,128)} %value_hbm.1, f32[2,128]{1,0:T(2,128)} %variance_hbm.1, f32[2,128,256]{2,1,0:T(8,128)} %noise_hbm.1), custom_call_target="tpu_custom_call" | custom-call | tf_op jit(solution)/shard_map/window/pallas_call | solution.py:523
  70.9 2.3 %copy.8 = bf16[32,64,256]{2,1,0:T(8,128)(2,1)} copy(bf16[32,64,256]{2,1,0:T(8,128)(2,1)} %window.1) | data formatting | bytes 2097152

commit v5 on v4

--- a/solution.py
+++ b/solution.py
@@ -8,6 +8,8 @@
 
 BATCHES = 2
 MESH = pl.DeviceIdType.MESH
+UNITS = 16
+BLOCK = 8
 VMEM_BYTES = 63 * 1024 * 1024
 LANES = 128
 HIGHEST = lax.Precision.HIGHEST
@@ -59,10 +61,11 @@
 
 
 def window_kernel(
-    sizes, state_hbm, courant_hbm, where_hbm, value_hbm, variance_hbm, noise_hbm, out_ref,
+    sizes, state_hbm, courant_hbm, where_hbm, value_hbm, variance_hbm, noise_hbm,
+    field_out, spread_out, change_ref,
     state_ref, courant_ref, where_ref, value_ref, variance_ref, noise_ref,
     near_ns, near_ew, near_corner, reach, wide, stencil, weights, part, pieces, piece, line, priors,
-    cells, bands, far_ns, far_ew, far_corner, field, spread, analysis,
+    cells, bands, far_ns, far_ew, far_corner, field, split, spread,
     in_sem, near_sem, far_sem, part_sem, line_sem, all_sem, send_sem, out_sem,
 ):
     lon_count, lat_count = sizes
@@ -292,7 +295,10 @@
         near_cells = cells[pl.ds(first, 6)].reshape(6 * LANES, members)
         result = jnp.dot(bands[...], near_cells, preferred_element_type=jnp.float32)
         for r in range(2):
-            field[first + r] = result[2 * r * cols : (2 * r + 1) * cols] + result[(2 * r + 1) * cols : (2 * r + 2) * cols]
+            value = result[2 * r * cols : (2 * r + 1) * cols] + result[(2 * r + 1) * cols : (2 * r + 2) * cols]
+            field[first + r] = value
+            at = pl.ds(pl.multiple_of((first + r) * cols, cols), cols)
+            split[at] = jnp.concatenate(halves_of(value), axis=1)
         return carry
 
     lax.fori_loop(0, rows // 2, one_pair_of_rows, 0)
@@ -311,7 +317,7 @@
         return priors[batch]
 
     analyse(
-        sizes, arrival, where_ref, value_ref, variance_ref, noise_ref, out_ref, field, spread, analysis, out_sem
+        sizes, arrival, where_ref, value_ref, variance_ref, noise_ref, field_out, spread_out, change_ref, field, split, spread, out_sem
     )
 
     for copy in near + far:
@@ -333,10 +339,20 @@
     return upper, (value - upper.astype(jnp.float32)).astype(jnp.bfloat16)
 
 
-def matmul_halves(left, right):
-    total = jnp.dot(left[0], right[1], preferred_element_type=jnp.float32)
-    total += jnp.dot(left[1], right[0], preferred_element_type=jnp.float32)
-    return total + jnp.dot(left[0], right[0], preferred_element_type=jnp.float32)
+def product(left, right):
+    return jnp.dot(left, right, preferred_element_type=jnp.float32)
+
+
+def twice(right):
+    upper, lower = halves_of(right)
+    return jnp.concatenate(
+        [jnp.concatenate([upper, lower], axis=1), jnp.concatenate([upper, jnp.zeros_like(lower)], axis=1)], axis=0
+    )
+
+
+def thrice(right):
+    upper, lower = halves_of(right)
+    return jnp.concatenate([upper, upper, lower], axis=0)
 
 
 def solve_pivot(pivot, rows):
@@ -370,7 +386,7 @@
     return terms[0]
 
 
-def inverse_of(system, panel=32):
+def inverse_of(system, beside, panel=32, block=8):
     size = system.shape[0]
     spread = (8, size)
     lane = lax.broadcasted_iota(jnp.int32, spread, 1)
@@ -381,28 +397,36 @@
     for start in range(0, size, panel):
         old = system[start : start + panel]
         bands = [old[i : i + 8] for i in range(0, panel, 8)]
-        for here in range(panel // 8):
+        for here in range(0, panel // 8, block // 8):
             first = start + 8 * here
-            inside = (lane >= first) & (lane < first + 8)
+            inside = (lane >= first) & (lane < first + block)
             columns = [
-                [jnp.broadcast_to(band[:, first + j : first + j + 1], spread) for j in range(8)] for band in bands
+                [jnp.broadcast_to(band[:, first + j : first + j + 1], spread) for j in range(block)] for band in bands
             ]
             pivot = {
-                (i, j): jnp.broadcast_to(columns[here][j][i : i + 1], spread) for i in range(8) for j in range(i + 1)
+                (i, j): jnp.broadcast_to(columns[here + i // 8][j][i % 8 : i % 8 + 1], spread)
+                for i in range(block)
+                for j in range(i + 1)
             }
             rows = [
-                jnp.where(inside, jnp.where(lane == first + j, -1.0, 0.0), jnp.broadcast_to(bands[here][j : j + 1], spread))
-                for j in range(8)
+                jnp.where(
+                    inside,
+                    jnp.where(lane == first + j, -1.0, 0.0),
+                    jnp.broadcast_to(bands[here + j // 8][j % 8 : j % 8 + 1], spread),
+                )
+                for j in range(block)
             ]
             rows = solve_pivot(pivot, rows)
             for i, band in enumerate(bands):
-                if i != here:
-                    terms = [columns[i][j] * rows[j] for j in range(8)]
+                if here <= i < here + block // 8:
+                    bands[i] = rows[8 * (i - here) + 7]
+                    for j in range(7):
+                        bands[i] = jnp.where(sub == j, rows[8 * (i - here) + j], bands[i])
+                else:
+                    terms = [columns[i][j] * rows[j] for j in range(block)]
                     bands[i] = jnp.where(inside, 0.0, band) - tree_sum(terms)
-            swept = rows[7]
-            for j in range(7):
-                swept = jnp.where(sub == j, rows[j], swept)
-            bands[here] = swept
+            for _ in range(block // 8):
+                beside()
         swept = jnp.concatenate(bands, axis=0)
         inside = (panel_lane >= start) & (panel_lane < start + panel)
         old = jnp.where(inside, jnp.where(panel_lane == panel_sub + start, -1.0, 0.0), old)
@@ -418,7 +442,7 @@
 
 
 def analyse(
-    sizes, arrival, where_ref, value_ref, variance_ref, noise_ref, out_ref, field, spread, analysis, out_sem
+    sizes, arrival, where_ref, value_ref, variance_ref, noise_ref, field_out, spread_out, change_ref, field, split, spread, out_sem
 ):
     lon_count, lat_count = sizes
     rows, cols, members = field.shape
@@ -437,12 +461,14 @@
     def scaled_square(gap, radius):
         return square(gap).astype(jnp.float32) / square(radius).astype(jnp.float32)
 
-    def weights_of(batch, priors, anomaly):
+    def weights_of(batch, priors, anomaly, unit):
         variance = upright[:, BATCHES + batch : BATCHES + batch + 1]
         system = matmul_exact(anomaly, anomaly, (1, 1)) / (members - 1)
         system += jnp.where(eye, variance, 0.0)
         misfit = upright[:, batch : batch + 1] + jnp.sqrt(variance) * noise_ref[batch] - priors
-        return matmul_exact(inverse_of(system), misfit)
+        units = iter(range(UNITS))
+        inverse = inverse_of(system, lambda: unit(next(units)), 32, BLOCK)
+        return matmul_exact(inverse, misfit)
 
     def centred(priors):
         return priors - jnp.mean(priors, axis=1, keepdims=True)
@@ -450,7 +476,30 @@
     obs = [[where_ref[i, batch : batch + 1, :] for i in range(3)] for batch in range(BATCHES)]
     priors = [arrival(0)]
     anomaly, weights = [centred(priors[0])], []
-    weights.append(weights_of(0, priors[0], anomaly[0]))
+    cell_lon = first_col + lax.broadcasted_iota(jnp.int32, (cols, 1), 0)
+    lon_part = [scaled_square(lon_distance(cell_lon, lon), radius) for _, lon, radius in obs]
+    count = rows // UNITS
+
+    def taper_of(batch, row):
+        lat, _, radius = obs[batch]
+        room = 1.0 - scaled_square(first_row + row - lat, radius)
+        return square(jnp.maximum(room - lon_part[batch], 0.0))
+
+    def spread_unit(batch, index, covariance):
+        covariance = covariance[:, :nobs] + covariance[:, nobs:]
+        taper = jnp.concatenate([taper_of(batch, index * count + r) for r in range(count)], axis=0)
+        upper, lower = halves_of(taper * covariance)
+        spread[batch, cells_of(index)] = jnp.concatenate([upper, lower, upper], axis=1)
+
+    def cells_of(index):
+        return pl.ds(index * count * cols, count * cols)
+
+    right = [twice(jnp.transpose(anomaly[0] / (members - 1)))]
+
+    def first_unit(index):
+        spread_unit(0, index, product(split[cells_of(index)], right[0]))
+
+    weights.append(weights_of(0, priors[0], anomaly[0], first_unit))
 
     where = jnp.concatenate(obs[1] + [jnp.zeros((8 - 3, nobs), jnp.int32)], axis=0)
     where = jnp.transpose(where.astype(jnp.float32)).astype(jnp.int32)
@@ -462,52 +511,80 @@
     covariance = matmul_exact(centred(before), anomaly[0], (1, 1)) / (members - 1)
     priors.append(before + matmul_exact(taper * covariance, weights[0]))
     anomaly.append(centred(priors[1]))
-    carried = halves_of(matmul_exact(centred(weights[0]), anomaly[1], (1, 1)) / (members - 1))
-
-    both = [jnp.transpose(part) for part in halves_of(jnp.concatenate(anomaly, axis=0) / (members - 1))]
-    cell_lon = first_col + lax.broadcasted_iota(jnp.int32, (cols, 1), 0)
-    lon_part = [scaled_square(lon_distance(cell_lon, lon), radius) for _, lon, radius in obs]
-    chunk = 4
-
-    def taper_of(batch, row):
-        lat, _, radius = obs[batch]
-        room = 1.0 - scaled_square(first_row + row - lat, radius)
-        return square(jnp.maximum(room - lon_part[batch], 0.0))
-
-    def spread_chunk(index, carry):
-        cells = field[pl.ds(index * chunk, chunk)].reshape(chunk * cols, members)
-        covariance = matmul_halves(halves_of(cells), both)
-        tapers = [
-            jnp.concatenate([taper_of(batch, index * chunk + r) for r in range(chunk)], axis=0)
-            for batch in range(BATCHES)
-        ]
-        first = tapers[0] * covariance[:, :nobs]
-        second = tapers[1] * (covariance[:, nobs:] + matmul_halves(halves_of(first), carried))
-        at = pl.ds(pl.multiple_of(index * chunk * cols, chunk * cols), chunk * cols)
-        for i, part in enumerate(halves_of(jnp.concatenate([first, second], axis=1))):
-            spread[i, at] = part
-        return carry
-
-    lax.fori_loop(0, rows // chunk, spread_chunk, 0)
-
-    weights.append(weights_of(1, priors[1], anomaly[1]))
-    both_weights = halves_of(jnp.concatenate(weights, axis=0))
-
-    def copy_out(index):
-        at = pl.ds(index * chunk, chunk)
-        return pltpu.make_async_copy(analysis.at[at], out_ref.at[at], out_sem.at[index])
-
-    def update_chunk(index, carry):
-        at = pl.ds(pl.multiple_of(index * chunk * cols, chunk * cols), chunk * cols)
-        change = matmul_halves((spread[0, at], spread[1, at]), both_weights)
-        at = pl.ds(index * chunk, chunk)
-        analysis[at] = (field[at] + change.reshape(chunk, cols, members)).astype(jnp.bfloat16)
-        copy_out(index).start()
-        return carry
-
-    lax.fori_loop(0, rows // chunk, update_chunk, 0)
-    for index in range(rows // chunk):
-        copy_out(index).wait()
+    carried = twice(matmul_exact(centred(weights[0]), anomaly[1], (1, 1)) / (members - 1))
+    right.append(twice(jnp.transpose(anomaly[1] / (members - 1))))
+    change = [thrice(weights[0])]
+
+    def second_unit(index):
+        at, at_rows = cells_of(index), pl.ds(index * count, count)
+        covariance = product(split[at], right[1]) + product(spread[0, at, : 2 * nobs], carried)
+        spread_unit(1, index, covariance)
+        field[at_rows] += product(spread[0, at], change[0]).reshape(count, cols, members)
+        for copy in copies_of(index):
+            copy.start()
+
+    def copies_of(index):
+        at, at_rows = cells_of(index), pl.ds(index * count, count)
+        return (
+            pltpu.make_async_copy(field.at[at_rows], field_out.at[at_rows], out_sem.at[index, 0]),
+            pltpu.make_async_copy(spread.at[1, at], spread_out.at[at], out_sem.at[index, 1]),
+        )
+
+    weights.append(weights_of(1, priors[1], anomaly[1], second_unit))
+    change.append(thrice(weights[1]))
+
+    change_ref[...] = change[1]
+    for index in range(UNITS):
+        for copy in copies_of(index):
+            copy.wait()
+
+
+def update_kernel(
+    field_hbm, spread_hbm, change_hbm, out_ref, field, spread, change, analysis, change_sem, in_sem, out_sem
+):
+    rows, cols, members = field.shape
+    chunks = out_sem.shape[0]
+    count = rows // chunks
+    whole = pltpu.make_async_copy(change_hbm, change, change_sem)
+    whole.start()
+    loads, stores = [], []
+    for index in range(chunks):
+        at, at_cells = pl.ds(index * count, count), pl.ds(index * count * cols, count * cols)
+        loads.append(
+            (
+                pltpu.make_async_copy(spread_hbm.at[at_cells], spread.at[at_cells], in_sem.at[index, 0]),
+                pltpu.make_async_copy(field_hbm.at[at], field.at[at], in_sem.at[index, 1]),
+            )
+        )
+        for load in loads[-1]:
+            load.start()
+    whole.wait()
+    for index in range(chunks):
+        at, at_cells = pl.ds(index * count, count), pl.ds(index * count * cols, count * cols)
+        for load in loads[index]:
+            load.wait()
+        step = product(spread[at_cells], change[...])
+        analysis[at] = (field[at] + step.reshape(count, cols, members)).astype(jnp.bfloat16)
+        stores.append(pltpu.make_async_copy(analysis.at[at], out_ref.at[at], out_sem.at[index]))
+        stores[-1].start()
+    for store in stores:
+        store.wait()
+
+
+def update(field, spread, change):
+    chunks = 8
+    anywhere = pl.BlockSpec(memory_space=pl.ANY)
+    dma = pltpu.SemaphoreType.DMA
+    return pl.pallas_call(
+        update_kernel,
+        out_shape=jax.ShapeDtypeStruct(field.shape, jnp.bfloat16),
+        in_specs=[anywhere] * 3,
+        out_specs=anywhere,
+        scratch_shapes=[pltpu.VMEM(array.shape, array.dtype) for array in (field, spread, change)]
+        + [pltpu.VMEM(field.shape, jnp.bfloat16), dma, dma((chunks, 2)), dma((chunks,))],
+        compiler_params=pltpu.CompilerParams(vmem_limit_bytes=VMEM_BYTES),
+        name="update",
+    )(field, spread, change)
 
 
 def window(state, courant, where, value, variance, noise, lon_count, lat_count):
@@ -522,9 +599,13 @@
     arguments = (state, courant, where, value, variance, noise)
     return pl.pallas_call(
         functools.partial(window_kernel, (lon_count, lat_count)),
-        out_shape=jax.ShapeDtypeStruct((rows, cols, members), bf16),
+        out_shape=(
+            jax.ShapeDtypeStruct((rows, cols, members), f32),
+            jax.ShapeDtypeStruct((rows * cols, 3 * nobs), bf16),
+            jax.ShapeDtypeStruct((3 * nobs, members), bf16),
+        ),
         in_specs=[anywhere] * len(arguments),
-        out_specs=anywhere,
+        out_specs=(anywhere, anywhere, pl.BlockSpec(memory_space=pltpu.VMEM)),
         scratch_shapes=[pltpu.VMEM(argument.shape, argument.dtype) for argument in arguments]
         + [
             pltpu.VMEM((2, 2, 8, cols), f32),
@@ -545,8 +626,8 @@
             pltpu.VMEM((4, rows, 2, members), f32),
             pltpu.VMEM((8, 8, members), f32),
             pltpu.VMEM((rows, cols, members), f32),
-            pltpu.VMEM((2, rows * cols, BATCHES * nobs), bf16),
-            pltpu.VMEM((rows, cols, members), bf16),
+            pltpu.VMEM((rows * cols, 2 * members), bf16),
+            pltpu.VMEM((BATCHES, rows * cols, 3 * nobs), bf16),
             dma((len(arguments),)),
             dma((8, 2)),
             dma((8, 2)),
@@ -554,7 +635,7 @@
             dma((BATCHES,)),
             dma((BATCHES,)),
             dma((BATCHES, 3)),
-            dma((rows // 4,)),
+            dma((UNITS, 2)),
         ],
         compiler_params=pltpu.CompilerParams(
             collective_id=0, has_side_effects=True, vmem_limit_bytes=VMEM_BYTES
@@ -566,7 +647,7 @@
 def body(ensemble_state, courant, obs_where, obs_value, obs_variance, obs_noise):
     counts = lax.axis_size("lon"), lax.axis_size("lat")
     where = jnp.transpose(obs_where, (1, 0, 2))
-    return window(ensemble_state, courant, where, obs_value, obs_variance, obs_noise, *counts)
+    return update(*window(ensemble_state, courant, where, obs_value, obs_variance, obs_noise, *counts))
 
 
 def solution(mesh):

time: 73.4 us -> 70.7 us (0.963)
  local copies, waits for them, and re-layouts: 2.3 us -> 0 us
    pallas_call x1, Pallas kernels: 70.9 us -> 65.2 us  [window(): pl.pallas_call(functools.partial(window_kernel, (lon_count, lat_count)),...]
    pallas_call x0 -> x1, Pallas kernels: none -> 5.2 us  [update(): pl.pallas_call(update_kernel, out_shape=jax.ShapeDtypeStruct(field.shape,...]
    unnamed x1 -> x0, local copies, waits for them, and re-layouts: 2.3 us -> none
where the time goes in v5:
time: 70.7 us; the launch traced here: 70.5 us
  Pallas kernels  70.4 us (100%)
    pallas_call x1, Pallas kernels, window(): pl.pallas_call(functools.partial(window_kernel, (lon_count, lat_count)),...  65.2 us
    pallas_call x1, Pallas kernels, update(): pl.pallas_call(update_kernel, out_shape=jax.ShapeDtypeStruct(field.shape,...  5.2 us

profile of v5, /device:TPU:1, one launch (start us, length us, event | category | flops | bytes accessed | tf_op | source)
XLA Modules:
  0.0 70.5 jit_solution(7325445801051883992)
XLA Ops:
  0.0 65.2 %window.1 = (f32[32,64,256]{2,1,0:T(8,128)}, bf16[2048,384]{1,0:T(8,128)(2,1)}, bf16[384,256]{1,0:T(8,128)(2,1)}) custom-call(bf16[32,64,256]{2,1,0:T(8,128)(2,1)} %state_hbm.1, f32[2,32,64]{2,1,0:T(8,128)} %courant_hbm.1, s32[3,2,128]{2,1,0:T(2,128)} %bitcast.1, f32[2,128]{1,0:T(2,128)} %value_hbm.1, f32[2,128]{1,0:T(2,128)} %variance_hbm.1, ...), custom_call_target="tpu_custom_call" | custom-call | tf_op jit(solution)/shard_map/window/pallas_call | solution.py:600
  65.2 5.2 %update.1 = bf16[32,64,256]{2,1,0:T(8,128)(2,1)} custom-call(f32[32,64,256]{2,1,0:T(8,128)} %get-tuple-element.8.field_hbm, bf16[2048,384]{1,0:T(8,128)(2,1)} %get-tuple-element.9.spread_hbm, bf16[384,256]{1,0:T(8,128)(2,1)} %get-tuple-element.10.change_hbm), custom_call_target="tpu_custom_call" | custom-call | tf_op jit(solution)/shard_map/update/pallas_call | solution.py:578

commit v6 on v5

--- a/solution.py
+++ b/solution.py
@@ -9,6 +9,7 @@
 BATCHES = 2
 MESH = pl.DeviceIdType.MESH
 UNITS = 16
+KEY = 8192
 BLOCK = 8
 VMEM_BYTES = 63 * 1024 * 1024
 LANES = 128
@@ -64,7 +65,7 @@
     sizes, state_hbm, courant_hbm, where_hbm, value_hbm, variance_hbm, noise_hbm,
     field_out, spread_out, change_ref,
     state_ref, courant_ref, where_ref, value_ref, variance_ref, noise_ref,
-    near_ns, near_ew, near_corner, reach, wide, stencil, weights, part, pieces, piece, line, priors,
+    near_ns, near_ew, near_corner, keys, reach, wide, stencil, weights, part, pieces, piece, line, priors,
     cells, bands, far_ns, far_ew, far_corner, field, split, spread,
     in_sem, near_sem, far_sem, part_sem, line_sem, all_sem, send_sem, out_sem,
 ):
@@ -142,6 +143,18 @@
             far_corner[2 * side + other] = state_ref[row, first : first + 8].astype(jnp.float32)
     cells[...] = jnp.zeros(cells.shape, jnp.bfloat16)
     cells[2 : 2 + rows, :cols] = state_ref[...]
+    flat_lane = lax.broadcasted_iota(jnp.int32, (nobs, LANES), 1)
+    second_row = jnp.where(flat_lane >= cols, 1, 0)
+    column = flat_lane - second_row * cols
+    for batch in range(BATCHES):
+        where = jnp.concatenate([where_ref[i, batch : batch + 1] for i in range(3)], axis=0)
+        where = jnp.concatenate([where, jnp.zeros((8 - 3, nobs), jnp.int32)], axis=0)
+        where = jnp.transpose(where.astype(jnp.float32)).astype(jnp.int32)
+        obs_row = where[:, 0:1] - lat * rows
+        obs_col = where[:, 1:2] - lon * cols + 2
+        obs_col = jnp.where(obs_col < 0, obs_col + total_cols, obs_col) - 2
+        obs_col = jnp.where(obs_col >= total_cols - 2, obs_col - total_cols, obs_col)
+        keys[batch] = (second_row - obs_row) * KEY + column - obs_col
     pl.semaphore_wait(barrier, len(greeted))
 
     def send(src, dst, sem, step):
@@ -218,32 +231,22 @@
         ref[at : at + count, columns] = upper
         ref[at + count : at + 2 * count, columns] = (value - upper.astype(jnp.float32)).astype(jnp.bfloat16)
 
-    flat_lane = lax.broadcasted_iota(jnp.int32, (nobs, LANES), 1)
-    second_row = jnp.where(flat_lane >= cols, 1, 0)
-    column = flat_lane - second_row * cols
     flat_state = state_ref[...].reshape(rows * cols, members)
-    for batch in range(BATCHES):
-        where = jnp.concatenate([where_ref[i, batch : batch + 1] for i in range(3)], axis=0)
-        where = jnp.concatenate([where, jnp.zeros((8 - 3, nobs), jnp.int32)], axis=0)
-        where = jnp.transpose(where.astype(jnp.float32)).astype(jnp.int32)
-        obs_row = where[:, 0:1] - lat * rows
-        obs_col = where[:, 1:2] - lon * cols + 2
-        obs_col = jnp.where(obs_col < 0, obs_col + total_cols, obs_col) - 2
-        obs_col = jnp.where(obs_col >= total_cols - 2, obs_col - total_cols, obs_col)
-        lon_step = column - obs_col
-        lat_base = second_row - obs_row
-
+
+    def make_share(batch):
         def one_pair(pair, carry):
-            lat_step = lat_base + 2 * pair
             total = jnp.zeros((nobs, LANES), jnp.float32)
             for index, (a, b) in enumerate(TWO_STEPS):
-                total = jnp.where((lat_step == a) & (lon_step == b), stencil[index, pl.ds(pair, 1), :], total)
+                met = keys[batch] == a * KEY + b - 2 * KEY * pair
+                total = jnp.where(met, stencil[index, pl.ds(pair, 1), :], total)
             halves_into(weights, 0, pl.ds(pl.multiple_of(pair * LANES, LANES), LANES), total)
             return carry
 
         lax.fori_loop(0, rows // 2, one_pair, 0)
         share = jnp.dot(weights[...], flat_state, preferred_element_type=jnp.float32)
         part[batch] = share[:nobs] + share[nobs:]
+
+    def send_share(batch):
         for index, partner in enumerate(partners):
             pltpu.make_async_remote_copy(
                 src_ref=part.at[batch, *tile_of(partner)], dst_ref=pieces.at[batch, index],
@@ -252,7 +255,8 @@
             ).start()
 
     mine = tile_of((0, 0))
-    for batch in range(BATCHES):
+
+    def send_piece(batch):
         pltpu.make_async_copy(pieces.at[batch], pieces.at[batch], part_sem.at[batch]).wait()
         piece[batch] = part[batch, *mine] + jnp.sum(pieces[batch], axis=0)
         for index, distance in enumerate(distances):
@@ -261,6 +265,22 @@
                 send_sem=send_sem.at[batch, 1], recv_sem=line_sem.at[batch],
                 device_id=line_device(distance), device_id_type=MESH,
             ).start()
+
+    def send_priors(batch):
+        pltpu.make_async_copy(line.at[batch], line.at[batch], line_sem.at[batch]).wait()
+        priors[batch, *mine] = piece[batch] + jnp.sum(line[batch], axis=0)
+        for partner in partners:
+            pltpu.make_async_remote_copy(
+                src_ref=priors.at[batch, *mine], dst_ref=priors.at[batch, *mine],
+                send_sem=send_sem.at[batch, 2], recv_sem=all_sem.at[batch],
+                device_id=plane_device(partner), device_id_type=MESH,
+            ).start()
+
+    make_share(0)
+    send_share(0)
+    make_share(1)
+    send_piece(0)
+    send_share(1)
 
     for copy in far:
         copy.wait_recv()
@@ -301,17 +321,12 @@
             split[at] = jnp.concatenate(halves_of(value), axis=1)
         return carry
 
-    lax.fori_loop(0, rows // 2, one_pair_of_rows, 0)
-
-    for batch in range(BATCHES):
-        pltpu.make_async_copy(line.at[batch], line.at[batch], line_sem.at[batch]).wait()
-        priors[batch, *mine] = piece[batch] + jnp.sum(line[batch], axis=0)
-        for partner in partners:
-            pltpu.make_async_remote_copy(
-                src_ref=priors.at[batch, *mine], dst_ref=priors.at[batch, *mine],
-                send_sem=send_sem.at[batch, 2], recv_sem=all_sem.at[batch],
-                device_id=plane_device(partner), device_id_type=MESH,
-            ).start()
+    lax.fori_loop(0, rows // 4, one_pair_of_rows, 0)
+    send_piece(1)
+    send_priors(0)
+    lax.fori_loop(rows // 4, rows // 2, one_pair_of_rows, 0)
+    send_priors(1)
+
     def arrival(batch):
         pltpu.make_async_copy(pieces.at[batch], pieces.at[batch], all_sem.at[batch]).wait()
         return priors[batch]
@@ -331,6 +346,24 @@
     return lax.dot_general(
         left, right, (((contract[0],), (contract[1],)), ((), ())),
         precision=HIGHEST, preferred_element_type=jnp.float32,
+    )
+
+
+def thirds_of(value):
+    upper = value.astype(jnp.bfloat16)
+    rest = value - upper.astype(jnp.float32)
+    middle = rest.astype(jnp.bfloat16)
+    return upper, middle, (rest - middle.astype(jnp.float32)).astype(jnp.bfloat16)
+
+
+def matmul_stacked(left, right, contract=(1, 0)):
+    a, b, c = thirds_of(left)
+    x, y, z = thirds_of(right)
+    return lax.dot_general(
+        jnp.concatenate([a, b, c, a, b, a], axis=contract[0]),
+        jnp.concatenate([z, y, x, y, x, x], axis=contract[1]),
+        (((contract[0],), (contract[1],)), ((), ())),
+        preferred_element_type=jnp.float32,
     )
 
 
@@ -431,7 +464,7 @@
         inside = (panel_lane >= start) & (panel_lane < start + panel)
         old = jnp.where(inside, jnp.where(panel_lane == panel_sub + start, -1.0, 0.0), old)
         inside = (whole_lane >= start) & (whole_lane < start + panel)
-        system = jnp.where(inside, 0.0, system) - matmul_exact(old, swept, (0, 0))
+        system = jnp.where(inside, 0.0, system) - matmul_stacked(old, swept, (0, 0))
         parts = [system[:start], swept, system[start + panel :]]
         system = jnp.concatenate([part for part in parts if part.shape[0]], axis=0)
     return -system
@@ -468,7 +501,7 @@
         misfit = upright[:, batch : batch + 1] + jnp.sqrt(variance) * noise_ref[batch] - priors
         units = iter(range(UNITS))
         inverse = inverse_of(system, lambda: unit(next(units)), 32, BLOCK)
-        return matmul_exact(inverse, misfit)
+        return matmul_stacked(inverse, misfit)
 
     def centred(priors):
         return priors - jnp.mean(priors, axis=1, keepdims=True)
@@ -509,7 +542,7 @@
     taper = square(jnp.maximum(1.0 - distance / square(obs[0][2]).astype(jnp.float32), 0.0))
     before = arrival(1)
     covariance = matmul_exact(centred(before), anomaly[0], (1, 1)) / (members - 1)
-    priors.append(before + matmul_exact(taper * covariance, weights[0]))
+    priors.append(before + matmul_stacked(taper * covariance, weights[0]))
     anomaly.append(centred(priors[1]))
     carried = twice(matmul_exact(centred(weights[0]), anomaly[1], (1, 1)) / (members - 1))
     right.append(twice(jnp.transpose(anomaly[1] / (members - 1))))
@@ -572,7 +605,7 @@
 
 
 def update(field, spread, change):
-    chunks = 8
+    chunks = 2
     anywhere = pl.BlockSpec(memory_space=pl.ANY)
     dma = pltpu.SemaphoreType.DMA
     return pl.pallas_call(
@@ -611,6 +644,7 @@
             pltpu.VMEM((2, 2, 8, cols), f32),
             pltpu.VMEM((2, 2, rows, cols), f32),
             pltpu.VMEM((4, 2, 8, cols), f32),
+            pltpu.VMEM((BATCHES, nobs, LANES), jnp.int32),
             pltpu.VMEM((2, rows + 16, LANES), f32),
             pltpu.VMEM((len(TWO_STEPS), rows + 16, LANES), f32),
             pltpu.VMEM((len(TWO_STEPS), rows // 2, LANES), f32),

time: 70.7 us -> 65 us (0.919)
  Pallas kernels: 70.4 us -> 64.9 us
    pallas_call x1, Pallas kernels: 65.2 us -> 60.9 us  [window(): pl.pallas_call(functools.partial(window_kernel, (lon_count, lat_count)),...]
    pallas_call x1, Pallas kernels: 5.2 us -> 3.96 us  [update(): pl.pallas_call(update_kernel, out_shape=jax.ShapeDtypeStruct(field.shape,...]
where the time goes in v6:
time: 65 us; the launch traced here: 64.9 us
  Pallas kernels  64.9 us (100%)
    pallas_call x1, Pallas kernels, window(): pl.pallas_call(functools.partial(window_kernel, (lon_count, lat_count)),...  60.9 us
    pallas_call x1, Pallas kernels, update(): pl.pallas_call(update_kernel, out_shape=jax.ShapeDtypeStruct(field.shape,...  3.96 us

profile of v6, /device:TPU:1, one launch (start us, length us, event | category | flops | bytes accessed | tf_op | source)
XLA Modules:
  0.0 64.9 jit_solution(3356379395091743561)
XLA Ops:
  0.0 60.9 %window.1 = (f32[32,64,256]{2,1,0:T(8,128)}, bf16[2048,384]{1,0:T(8,128)(2,1)}, bf16[384,256]{1,0:T(8,128)(2,1)}) custom-call(bf16[32,64,256]{2,1,0:T(8,128)(2,1)} %state_hbm.1, f32[2,32,64]{2,1,0:T(8,128)} %courant_hbm.1, s32[3,2,128]{2,1,0:T(2,128)} %bitcast.1, f32[2,128]{1,0:T(2,128)} %value_hbm.1, f32[2,128]{1,0:T(2,128)} %variance_hbm.1, ...), custom_call_target="tpu_custom_call" | custom-call | tf_op jit(solution)/shard_map/window/pallas_call | solution.py:633
  60.9 4.0 %update.1 = bf16[32,64,256]{2,1,0:T(8,128)(2,1)} custom-call(f32[32,64,256]{2,1,0:T(8,128)} %get-tuple-element.8.field_hbm, bf16[2048,384]{1,0:T(8,128)(2,1)} %get-tuple-element.9.spread_hbm, bf16[384,256]{1,0:T(8,128)(2,1)} %get-tuple-element.10.change_hbm), custom_call_target="tpu_custom_call" | custom-call | tf_op jit(solution)/shard_map/update/pallas_call | solution.py:611

commit v7 on v6

--- a/solution.py
+++ b/solution.py
@@ -63,10 +63,10 @@
 
 def window_kernel(
     sizes, state_hbm, courant_hbm, where_hbm, value_hbm, variance_hbm, noise_hbm,
-    field_out, spread_out, change_ref,
+    out_ref,
     state_ref, courant_ref, where_ref, value_ref, variance_ref, noise_ref,
     near_ns, near_ew, near_corner, keys, reach, wide, stencil, weights, part, pieces, piece, line, priors,
-    cells, bands, far_ns, far_ew, far_corner, field, split, spread,
+    cells, bands, far_ns, far_ew, far_corner, field, split, spread, analysis,
     in_sem, near_sem, far_sem, part_sem, line_sem, all_sem, send_sem, out_sem,
 ):
     lon_count, lat_count = sizes
@@ -157,6 +157,9 @@
         keys[batch] = (second_row - obs_row) * KEY + column - obs_col
     pl.semaphore_wait(barrier, len(greeted))
 
+    def has(lat_step):
+        return (lat + lat_step >= 0) & (lat + lat_step < lat_count)
+
     def send(src, dst, sem, step):
         copy = pltpu.make_async_remote_copy(
             src_ref=src, dst_ref=dst, send_sem=sem.at[0], recv_sem=sem.at[1],
@@ -186,7 +189,17 @@
             source, target = far_ns.at[up], far_ns.at[2 + 1 - up]
         else:
             source, target = far_ew.at[right], far_ew.at[2 + 1 - right]
-        far.append(send(source, target, far_sem.at[index], (a, b)))
+        far.append(
+            (
+                pltpu.make_async_remote_copy(
+                    src_ref=source, dst_ref=target, send_sem=far_sem.at[index, 0], recv_sem=far_sem.at[index, 1],
+                    device_id=neighbour(a, b), device_id_type=MESH,
+                ),
+                (a, b),
+            )
+        )
+    for copy, (a, _) in far:
+        pl.when(has(a))(copy.start)
     for copy in near:
         copy.wait_recv()
 
@@ -282,8 +295,6 @@
     send_piece(0)
     send_share(1)
 
-    for copy in far:
-        copy.wait_recv()
     gap = jnp.zeros((14, members), jnp.float32)
 
     def beside(at, west, east):
@@ -294,10 +305,10 @@
         beside(r + 2, far_ew[2, r], far_ew[3, r])
         return carry
 
+    for copy, (a, _) in far:
+        if a == 0:
+            copy.wait_recv()
     lax.fori_loop(0, rows, beside_row, 0)
-    for side, at in ((0, 1), (1, rows + 2)):
-        cells[(0, rows + 2)[side] : (2, rows + 4)[side], :cols] = far_ns[2 + side].astype(jnp.bfloat16)
-        beside(at, far_corner[4 + 2 * side, 6:8], far_corner[4 + 2 * side + 1, 0:2])
     step_lane = lax.broadcasted_iota(jnp.int32, (cols, LANES), 1) - lax.broadcasted_iota(jnp.int32, (cols, LANES), 0)
     step_lane = jnp.where(step_lane > LANES // 2 + 2, step_lane - LANES, step_lane)
 
@@ -321,10 +332,21 @@
             split[at] = jnp.concatenate(halves_of(value), axis=1)
         return carry
 
-    lax.fori_loop(0, rows // 4, one_pair_of_rows, 0)
+    lax.fori_loop(1, rows // 4, one_pair_of_rows, 0)
     send_piece(1)
     send_priors(0)
-    lax.fori_loop(rows // 4, rows // 2, one_pair_of_rows, 0)
+    lax.fori_loop(rows // 4, rows // 2 - 1, one_pair_of_rows, 0)
+    for copy, (a, _) in far:
+        if a:
+            pl.when(has(-a))(copy.wait_recv)
+    for side, at in ((0, 1), (1, rows + 2)):
+
+        @pl.when(has((-1, 1)[side]))
+        def _(side=side, at=at):
+            cells[(0, rows + 2)[side] : (2, rows + 4)[side], :cols] = far_ns[2 + side].astype(jnp.bfloat16)
+            beside(at, far_corner[4 + 2 * side, 6:8], far_corner[4 + 2 * side + 1, 0:2])
+
+    lax.fori_loop(0, 2, lambda end, carry: one_pair_of_rows(end * (rows // 2 - 1), carry), 0)
     send_priors(1)
 
     def arrival(batch):
@@ -332,11 +354,13 @@
         return priors[batch]
 
     analyse(
-        sizes, arrival, where_ref, value_ref, variance_ref, noise_ref, field_out, spread_out, change_ref, field, split, spread, out_sem
+        sizes, arrival, where_ref, value_ref, variance_ref, noise_ref, out_ref, field, split, spread, analysis, out_sem
     )
 
-    for copy in near + far:
+    for copy in near:
         copy.wait_send()
+    for copy, (a, _) in far:
+        pl.when(has(a))(copy.wait_send)
     for batch in range(BATCHES):
         for sem, sent in enumerate((pieces, line, pieces)):
             pltpu.make_async_copy(sent.at[batch], sent.at[batch], send_sem.at[batch, sem]).wait()
@@ -475,7 +499,7 @@
 
 
 def analyse(
-    sizes, arrival, where_ref, value_ref, variance_ref, noise_ref, field_out, spread_out, change_ref, field, split, spread, out_sem
+    sizes, arrival, where_ref, value_ref, variance_ref, noise_ref, out_ref, field, split, spread, analysis, out_sem
 ):
     lon_count, lat_count = sizes
     rows, cols, members = field.shape
@@ -553,71 +577,21 @@
         covariance = product(split[at], right[1]) + product(spread[0, at, : 2 * nobs], carried)
         spread_unit(1, index, covariance)
         field[at_rows] += product(spread[0, at], change[0]).reshape(count, cols, members)
-        for copy in copies_of(index):
-            copy.start()
-
-    def copies_of(index):
-        at, at_rows = cells_of(index), pl.ds(index * count, count)
-        return (
-            pltpu.make_async_copy(field.at[at_rows], field_out.at[at_rows], out_sem.at[index, 0]),
-            pltpu.make_async_copy(spread.at[1, at], spread_out.at[at], out_sem.at[index, 1]),
-        )
 
     weights.append(weights_of(1, priors[1], anomaly[1], second_unit))
     change.append(thrice(weights[1]))
 
-    change_ref[...] = change[1]
-    for index in range(UNITS):
-        for copy in copies_of(index):
-            copy.wait()
-
-
-def update_kernel(
-    field_hbm, spread_hbm, change_hbm, out_ref, field, spread, change, analysis, change_sem, in_sem, out_sem
-):
-    rows, cols, members = field.shape
+    stores = []
     chunks = out_sem.shape[0]
-    count = rows // chunks
-    whole = pltpu.make_async_copy(change_hbm, change, change_sem)
-    whole.start()
-    loads, stores = [], []
+    count_out = rows // chunks
     for index in range(chunks):
-        at, at_cells = pl.ds(index * count, count), pl.ds(index * count * cols, count * cols)
-        loads.append(
-            (
-                pltpu.make_async_copy(spread_hbm.at[at_cells], spread.at[at_cells], in_sem.at[index, 0]),
-                pltpu.make_async_copy(field_hbm.at[at], field.at[at], in_sem.at[index, 1]),
-            )
-        )
-        for load in loads[-1]:
-            load.start()
-    whole.wait()
-    for index in range(chunks):
-        at, at_cells = pl.ds(index * count, count), pl.ds(index * count * cols, count * cols)
-        for load in loads[index]:
-            load.wait()
-        step = product(spread[at_cells], change[...])
-        analysis[at] = (field[at] + step.reshape(count, cols, members)).astype(jnp.bfloat16)
+        at = pl.ds(index * count_out, count_out)
+        step = product(spread[1, pl.ds(index * count_out * cols, count_out * cols)], change[1])
+        analysis[at] = (field[at] + step.reshape(count_out, cols, members)).astype(jnp.bfloat16)
         stores.append(pltpu.make_async_copy(analysis.at[at], out_ref.at[at], out_sem.at[index]))
         stores[-1].start()
     for store in stores:
         store.wait()
-
-
-def update(field, spread, change):
-    chunks = 2
-    anywhere = pl.BlockSpec(memory_space=pl.ANY)
-    dma = pltpu.SemaphoreType.DMA
-    return pl.pallas_call(
-        update_kernel,
-        out_shape=jax.ShapeDtypeStruct(field.shape, jnp.bfloat16),
-        in_specs=[anywhere] * 3,
-        out_specs=anywhere,
-        scratch_shapes=[pltpu.VMEM(array.shape, array.dtype) for array in (field, spread, change)]
-        + [pltpu.VMEM(field.shape, jnp.bfloat16), dma, dma((chunks, 2)), dma((chunks,))],
-        compiler_params=pltpu.CompilerParams(vmem_limit_bytes=VMEM_BYTES),
-        name="update",
-    )(field, spread, change)
 
 
 def window(state, courant, where, value, variance, noise, lon_count, lat_count):
@@ -632,13 +606,9 @@
     arguments = (state, courant, where, value, variance, noise)
     return pl.pallas_call(
         functools.partial(window_kernel, (lon_count, lat_count)),
-        out_shape=(
-            jax.ShapeDtypeStruct((rows, cols, members), f32),
-            jax.ShapeDtypeStruct((rows * cols, 3 * nobs), bf16),
-            jax.ShapeDtypeStruct((3 * nobs, members), bf16),
-        ),
+        out_shape=jax.ShapeDtypeStruct((rows, cols, members), bf16),
         in_specs=[anywhere] * len(arguments),
-        out_specs=(anywhere, anywhere, pl.BlockSpec(memory_space=pltpu.VMEM)),
+        out_specs=anywhere,
         scratch_shapes=[pltpu.VMEM(argument.shape, argument.dtype) for argument in arguments]
         + [
             pltpu.VMEM((2, 2, 8, cols), f32),
@@ -662,6 +632,7 @@
             pltpu.VMEM((rows, cols, members), f32),
             pltpu.VMEM((rows * cols, 2 * members), bf16),
             pltpu.VMEM((BATCHES, rows * cols, 3 * nobs), bf16),
+            pltpu.VMEM((rows, cols, members), bf16),
             dma((len(arguments),)),
             dma((8, 2)),
             dma((8, 2)),
@@ -669,7 +640,7 @@
             dma((BATCHES,)),
             dma((BATCHES,)),
             dma((BATCHES, 3)),
-            dma((UNITS, 2)),
+            dma((4,)),
         ],
         compiler_params=pltpu.CompilerParams(
             collective_id=0, has_side_effects=True, vmem_limit_bytes=VMEM_BYTES
@@ -681,7 +652,7 @@
 def body(ensemble_state, courant, obs_where, obs_value, obs_variance, obs_noise):
     counts = lax.axis_size("lon"), lax.axis_size("lat")
     where = jnp.transpose(obs_where, (1, 0, 2))
-    return update(*window(ensemble_state, courant, where, obs_value, obs_variance, obs_noise, *counts))
+    return window(ensemble_state, courant, where, obs_value, obs_variance, obs_noise, *counts)
 
 
 def solution(mesh):

time: 65 us -> 63.1 us (0.971)
  Pallas kernels: 64.9 us -> 60.6 us
  local copies, waits for them, and re-layouts: 0 us -> 2.3 us
    pallas_call x1 -> x0, Pallas kernels: 3.96 us -> none  [update(): pl.pallas_call(update_kernel, out_shape=jax.ShapeDtypeStruct(field.shape,...]
    unnamed x0 -> x1, local copies, waits for them, and re-layouts: none -> 2.3 us
where the time goes in v7:
time: 63.1 us; the launch traced here: 62.9 us
  Pallas kernels  60.6 us (96%)
  local copies, waits for them, and re-layouts  2.3 us (4%)
    pallas_call x1, Pallas kernels, window(): pl.pallas_call(functools.partial(window_kernel, (lon_count, lat_count)),...  60.6 us
    unnamed x1, local copies, waits for them, and re-layouts  2.3 us

profile of v7, /device:TPU:1, one launch (start us, length us, event | category | flops | bytes accessed | tf_op | source)
XLA Modules:
  0.0 62.9 jit_solution(7063239898036740283)
XLA Ops:
  0.0 60.6 %window.1 = bf16[32,64,256]{2,1,0:T(8,128)(2,1)} custom-call(bf16[32,64,256]{2,1,0:T(8,128)(2,1)} %state_hbm.1, f32[2,32,64]{2,1,0:T(8,128)} %courant_hbm.1, s32[3,2,128]{2,1,0:T(2,128)} %bitcast.1, f32[2,128]{1,0:T(2,128)} %value_hbm.1, f32[2,128]{1,0:T(2,128)} %variance_hbm.1, f32[2,128,256]{2,1,0:T(8,128)} %noise_hbm.1), custom_call_target="tpu_custom_call" | custom-call | tf_op jit(solution)/shard_map/window/pallas_call | solution.py:607
  60.6 2.3 %copy.8 = bf16[32,64,256]{2,1,0:T(8,128)(2,1)} copy(bf16[32,64,256]{2,1,0:T(8,128)(2,1)} %window.1) | data formatting | bytes 2097152

commit v8 on v7

--- a/solution.py
+++ b/solution.py
@@ -525,7 +525,8 @@
         misfit = upright[:, batch : batch + 1] + jnp.sqrt(variance) * noise_ref[batch] - priors
         units = iter(range(UNITS))
         inverse = inverse_of(system, lambda: unit(next(units)), 32, BLOCK)
-        return matmul_stacked(inverse, misfit)
+        both = matmul_stacked(inverse, jnp.concatenate([misfit, centred(misfit)], axis=1))
+        return both[:, :members], both[:, members:]
 
     def centred(priors):
         return priors - jnp.mean(priors, axis=1, keepdims=True)
@@ -553,22 +554,29 @@
 
     right = [twice(jnp.transpose(anomaly[0] / (members - 1)))]
 
-    def first_unit(index):
-        spread_unit(0, index, product(split[cells_of(index)], right[0]))
-
-    weights.append(weights_of(0, priors[0], anomaly[0], first_unit))
-
     where = jnp.concatenate(obs[1] + [jnp.zeros((8 - 3, nobs), jnp.int32)], axis=0)
     where = jnp.transpose(where.astype(jnp.float32)).astype(jnp.int32)
     lat_gap = where[:, 0:1] - obs[0][0]
     lon_gap = lon_distance(where[:, 1:2], obs[0][1])
     distance = (square(lat_gap) + square(lon_gap)).astype(jnp.float32)
     taper = square(jnp.maximum(1.0 - distance / square(obs[0][2]).astype(jnp.float32), 0.0))
-    before = arrival(1)
-    covariance = matmul_exact(centred(before), anomaly[0], (1, 1)) / (members - 1)
-    priors.append(before + matmul_stacked(taper * covariance, weights[0]))
-    anomaly.append(centred(priors[1]))
-    carried = twice(matmul_exact(centred(weights[0]), anomaly[1], (1, 1)) / (members - 1))
+    later = []
+
+    def first_unit(index):
+        if index == UNITS - 1:
+            before = arrival(1)
+            covariance = matmul_exact(centred(before), anomaly[0], (1, 1)) / (members - 1)
+            later.extend((before, taper * covariance))
+        spread_unit(0, index, product(split[cells_of(index)], right[0]))
+
+    first_weights = weights_of(0, priors[0], anomaly[0], first_unit)
+    weights.append(first_weights[0])
+
+    before, tapered = later
+    change = matmul_stacked(tapered, jnp.concatenate(first_weights, axis=1))
+    priors.append(before + change[:, :members])
+    anomaly.append(centred(before) + change[:, members:])
+    carried = twice(matmul_exact(first_weights[1], anomaly[1], (1, 1)) / (members - 1))
     right.append(twice(jnp.transpose(anomaly[1] / (members - 1))))
     change = [thrice(weights[0])]
 
@@ -578,7 +586,7 @@
         spread_unit(1, index, covariance)
         field[at_rows] += product(spread[0, at], change[0]).reshape(count, cols, members)
 
-    weights.append(weights_of(1, priors[1], anomaly[1], second_unit))
+    weights.append(weights_of(1, priors[1], anomaly[1], second_unit)[0])
     change.append(thrice(weights[1]))
 
     stores = []

time: 63.1 us -> 63.3 us (level)
  no operation moved by 1% of the time
where the time goes in v8:
time: 63.3 us; the launch traced here: 63.1 us
  Pallas kernels  60.8 us (96%)
  local copies, waits for them, and re-layouts  2.3 us (4%)
    pallas_call x1, Pallas kernels, window(): pl.pallas_call(functools.partial(window_kernel, (lon_count, lat_count)),...  60.8 us
    unnamed x1, local copies, waits for them, and re-layouts  2.3 us

profile of v8, /device:TPU:1, one launch (start us, length us, event | category | flops | bytes accessed | tf_op | source)
XLA Modules:
  0.0 63.1 jit_solution(16047870129898429795)
XLA Ops:
  0.0 60.8 %window.1 = bf16[32,64,256]{2,1,0:T(8,128)(2,1)} custom-call(bf16[32,64,256]{2,1,0:T(8,128)(2,1)} %state_hbm.1, f32[2,32,64]{2,1,0:T(8,128)} %courant_hbm.1, s32[3,2,128]{2,1,0:T(2,128)} %bitcast.1, f32[2,128]{1,0:T(2,128)} %value_hbm.1, f32[2,128]{1,0:T(2,128)} %variance_hbm.1, f32[2,128,256]{2,1,0:T(8,128)} %noise_hbm.1), custom_call_target="tpu_custom_call" | custom-call | tf_op jit(solution)/shard_map/window/pallas_call | solution.py:615
  60.8 2.3 %copy.8 = bf16[32,64,256]{2,1,0:T(8,128)(2,1)} copy(bf16[32,64,256]{2,1,0:T(8,128)(2,1)} %window.1) | data formatting | bytes 2097152
